TPU v7x, 256 devices: a whole 4x4x8 slice. The times are simulated.
256 devices in a mesh: gz: 4 (over y), gx: 16 (over x, z_hi), gy: 4 (over z_lo, core).
Axes of the slice: x: 4, y: 4, z: 8 (z_hi: 4, z_lo: 2; z = z_hi * 2 + z_lo), core: 2. Of those that a mesh axis runs over, the one named last changes fastest.
Arguments:
- potential: float32 [4, 32, 512, 1024], P(None, 'gz', 'gx', 'gy'), may hold values from -4 to 4
- labels: int32 [32, 512, 1024], P('gz', 'gx', 'gy'), may hold values from 0 to 15
- conductivity: float32 [16], replicated, may hold values from 0.1 to 10
- electrodes: int32 [4, 4], replicated, may hold values from 0 to 511
Outputs:
- relaxed: float32 [4, 32, 512, 1024], P(None, 'gz', 'gx', 'gy')
- coarse_residual: float32 [4, 32, 256, 512], P(None, 'gz', 'gx', 'gy')
All inputs are finite; a program needn't handle non-finite values.
Results may differ from a plain program's by a relative error of at most 0.0003.
Values sent between devices are 32-bit elements; how exact they have to be, the bound alone decides.
A program may use at most 128 MiB of HBM per device.

v0:
```python
import jax
import jax.numpy as jnp
from jax import lax
from jax.sharding import PartitionSpec as P

ASPECT = 128


def with_halo(cells, sides, width):
    for axis, dim in sides:
        count = lax.axis_size(axis)
        ends = count - 1
        head = lax.slice_in_dim(cells, 0, width, axis=dim)
        tail = lax.slice_in_dim(cells, cells.shape[dim] - width, cells.shape[dim], axis=dim)
        cells = jnp.concatenate(
            [
                lax.ppermute(tail, axis, [(i, (i + 1) % count) for i in range(ends)]),
                cells,
                lax.ppermute(head, axis, [((i + 1) % count, i) for i in range(ends)]),
            ],
            axis=dim,
        )
    return cells


def harmonic(first_value, second_value):
    summed = first_value + second_value
    return 2.0 * first_value * second_value / jnp.where(summed > 0, summed, 1.0)


def trimmed(item_array, margin):
    if isinstance(item_array, float) or margin == 0:
        return item_array
    return item_array[
        ..., margin : item_array.shape[-2] - margin, margin : item_array.shape[-1] - margin
    ]


def lookup(labels, conductivity):
    sigma_cells = jnp.zeros(labels.shape, jnp.float32)
    for label_index in range(conductivity.shape[0]):
        sigma_cells = sigma_cells + jnp.where(labels == label_index, conductivity[label_index], 0.0)
    return sigma_cells


def face_links(stacked, last_part):
    depth_weight = float(ASPECT * ASPECT)
    inner_rows = stacked[1:-1]
    top_rows = jnp.where(last_part, inner_rows[-1:], stacked[-1:])
    full_rows = jnp.concatenate([stacked[:1], inner_rows, top_rows], 0)
    middle = full_rows[1:-1, 1:-1, 1:-1]
    link_shallow = depth_weight * harmonic(full_rows[:-2, 1:-1, 1:-1], middle)
    link_deep = depth_weight * harmonic(full_rows[2:, 1:-1, 1:-1], middle)
    link_west = harmonic(full_rows[1:-1, :-2, 1:-1], middle)
    link_east = harmonic(full_rows[1:-1, 2:, 1:-1], middle)
    link_south = harmonic(full_rows[1:-1, 1:-1, :-2], middle)
    link_north = harmonic(full_rows[1:-1, 1:-1, 2:], middle)
    diagonal = link_shallow + link_deep + link_west + link_east + link_south + link_north
    diagonal = jnp.where(middle > 0, diagonal, 1.0)
    return (link_shallow, link_deep, link_west, link_east, link_south, link_north, diagonal)


def lateral(grid_field, link_west, link_east, link_south, link_north):
    return (
        link_west * grid_field[:, :, :-2, 1:-1]
        + link_east * grid_field[:, :, 2:, 1:-1]
        + (link_south * grid_field[:, :, 1:-1, :-2] + link_north * grid_field[:, :, 1:-1, 2:])
    )


def side_rims(grid_field):
    return with_halo(grid_field, (("gx", 2), ("gy", 3)), 1)


def source_field(electrodes, halo_rim, depth_cells, width_x, width_y, first_part):
    strength = 4.0 * ASPECT
    x_cells = (
        lax.axis_index("gx") * width_x
        - halo_rim
        + jnp.arange(width_x + 2 * halo_rim, dtype=jnp.int32)
    )
    y_cells = (
        lax.axis_index("gy") * width_y
        - halo_rim
        + jnp.arange(width_y + 2 * halo_rim, dtype=jnp.int32)
    )
    x_grid = x_cells[None, :, None]
    y_grid = y_cells[None, None, :]
    hit_first = (
        (x_grid == electrodes[:, 0, None, None]) & (y_grid == electrodes[:, 1, None, None])
    ).astype(jnp.float32)
    hit_second = (
        (x_grid == electrodes[:, 2, None, None]) & (y_grid == electrodes[:, 3, None, None])
    ).astype(jnp.float32)
    surface = strength * (hit_first - hit_second)
    surface = jnp.where(first_part, surface, 0.0)
    below_rows = jnp.zeros((surface.shape[0], depth_cells - 1) + surface.shape[1:], jnp.float32)
    return jnp.concatenate([surface[:, None], below_rows], 1)


def factor_block(link_shallow, link_deep, diagonal):
    ratios = []
    denoms = []
    for row_index in range(diagonal.shape[0]):
        if row_index == 0:
            denominator = diagonal[0]
        else:
            denominator = diagonal[row_index] - link_shallow[row_index] * ratios[-1]
        denoms.append(denominator)
        ratios.append(link_deep[row_index] / denominator)
    return (ratios, denoms)


def solve_block(link_shallow, ratios, denoms, right_side):
    forward_values = []
    for row_index in range(len(denoms)):
        if row_index == 0:
            running = right_side[:, 0]
        else:
            running = right_side[:, row_index] + link_shallow[row_index] * forward_values[-1]
        forward_values.append(running / denoms[row_index])
    solved = [forward_values[-1]]
    for row_index in range(len(denoms) - 2, -1, -1):
        solved.append(forward_values[row_index] + ratios[row_index] * solved[-1])
    return jnp.stack(solved[::-1], 1)


def block_spreads(link_shallow, link_deep, ratios, denoms):
    zero_rows = jnp.zeros((link_shallow.shape[0] - 1,) + link_shallow.shape[1:], jnp.float32)
    from_shallow = jnp.concatenate([link_shallow[:1], zero_rows], 0)
    from_deep = jnp.concatenate([zero_rows, link_deep[-1:]], 0)
    return solve_block(link_shallow, ratios, denoms, jnp.stack([from_shallow, from_deep], 0))


def spread_ends(spreads):
    return jnp.stack([spreads[0, 0], spreads[0, -1], spreads[1, 0], spreads[1, -1]], 0)[None]


def value_ends(local_part):
    return jnp.stack([local_part[:, 0], local_part[:, -1]], 1)[None]


def eliminate(spread_rows, part_count):
    system_size = 2 * part_count
    matrix = [[0.0] * system_size for matrix_row in range(system_size)]
    for block_index in range(part_count):
        for offset in range(2):
            row_index = 2 * block_index + offset
            matrix[row_index][row_index] = 1.0
            if block_index > 0:
                matrix[row_index][2 * block_index - 1] = -spread_rows[block_index, offset]
            if block_index < part_count - 1:
                matrix[row_index][2 * block_index + 2] = -spread_rows[block_index, 2 + offset]
    factors = []
    for pivot_row in range(system_size):
        pivot_value = matrix[pivot_row][pivot_row]
        for target_row in range(pivot_row + 1, min(system_size, pivot_row + 3)):
            entry_value = matrix[target_row][pivot_row]
            if isinstance(entry_value, float):
                continue
            factor = entry_value / pivot_value
            factors.append((target_row, pivot_row, factor))
            for column in range(pivot_row + 1, min(system_size, pivot_row + 3)):
                upper_entry = matrix[pivot_row][column]
                if not isinstance(upper_entry, float):
                    matrix[target_row][column] = matrix[target_row][column] - factor * upper_entry
    return (factors, matrix)


def substitute(factors, matrix, values):
    values = list(values)
    for target_row, pivot_row, factor in factors:
        values[target_row] = values[target_row] - factor * values[pivot_row]
    system_size = len(values)
    solution = [None] * system_size
    for row_index in range(system_size - 1, -1, -1):
        running = values[row_index]
        for column in range(row_index + 1, min(system_size, row_index + 3)):
            entry_value = matrix[row_index][column]
            if not isinstance(entry_value, float):
                running = running - entry_value * solution[column]
        solution[row_index] = running / matrix[row_index][row_index]
    return solution


def connect(local_part, spreads, factors, matrix, value_rows, part_count, part_index):
    values = []
    for block_index in range(part_count):
        values.append(value_rows[block_index, :, 0])
        values.append(value_rows[block_index, :, 1])
    solution = substitute(factors, matrix, values)
    zero_slab = jnp.zeros_like(solution[0])
    padded = jnp.stack([zero_slab] + solution + [zero_slab], 0)
    from_shallow = lax.dynamic_index_in_dim(padded, 2 * part_index, 0, keepdims=False)
    from_deep = lax.dynamic_index_in_dim(padded, 2 * part_index + 3, 0, keepdims=False)
    return (
        local_part
        + spreads[0][None] * from_shallow[:, None]
        + spreads[1][None] * from_deep[:, None]
    )


def body(potential, labels, conductivity, electrodes):
    source_count, depth_cells, width_x, width_y = potential.shape
    part_count = lax.axis_size("gz")
    part_index = lax.axis_index("gz")
    first_part = part_index == 0
    last_part = part_index == part_count - 1
    sigma_cells = lookup(labels, conductivity)
    halo_depth = 1
    sigma_sides = with_halo(sigma_cells, (("gx", 1), ("gy", 2)), 1)
    stacked = with_halo(sigma_sides, (("gz", 0),), 1)
    face_set = face_links(stacked, last_part)
    widest = halo_depth - 1

    def relax(grid_field, out_rim):
        margin = widest - out_rim
        link_shallow, link_deep, link_west, link_east, link_south, link_north, diagonal = [
            trimmed(entry_item, margin) for entry_item in face_set
        ]
        right_side = source_field(
            electrodes, out_rim, depth_cells, width_x, width_y, first_part
        ) + lateral(grid_field, link_west, link_east, link_south, link_north)
        ratios, denoms = factor_block(link_shallow, link_deep, diagonal)
        spreads = block_spreads(link_shallow, link_deep, ratios, denoms)
        local_part = solve_block(link_shallow, ratios, denoms, right_side)
        spread_rows, value_rows = (
            lax.all_gather(spread_ends(spreads), "gz", axis=0, tiled=True),
            lax.all_gather(value_ends(local_part), "gz", axis=0, tiled=True),
        )
        factors, matrix = eliminate(spread_rows, part_count)
        return connect(local_part, spreads, factors, matrix, value_rows, part_count, part_index)

    first_pass = relax(side_rims(potential), 0)
    relaxed = relax(side_rims(first_pass), 0)
    change = side_rims(relaxed - first_pass)
    defect = lateral(
        change,
        trimmed(face_set[2], widest),
        trimmed(face_set[3], widest),
        trimmed(face_set[4], widest),
        trimmed(face_set[5], widest),
    )
    coarse_residual = defect.reshape(
        source_count, depth_cells, width_x // 2, 2, width_y // 2, 2
    ).sum(axis=(3, 5))
    return (relaxed, coarse_residual)


def solution(mesh):
    return jax.shard_map(
        body,
        mesh=mesh,
        in_specs=(P(None, "gz", "gx", "gy"), P("gz", "gx", "gy"), P(), P()),
        out_specs=(P(None, "gz", "gx", "gy"), P(None, "gz", "gx", "gy")),
        check_vma=False,
    )
```

profile of v0, /device:TPU:6, one launch (start us, length us, event | category | flops | bytes accessed | tf_op | source)
XLA Modules:
  0.0 259.8 jit_solution(17967812393826052805)
XLA Ops:
  7.2 1.9 copy.176
  9.1 8.6 %collective-permute-start.3 = (f32[4,8,1,256]{3,1,2,0:T(8,128)S(1)}, f32[4,8,1,256]{3,1,2,0:T(8,128)S(1)}, u32[]{:S(2)}, u32[]{:S(2)}) collective-permute-start(f32[4,8,1,256]{3,1,2,0:T(8,128)S(1)} %get-tuple-element.109), channel_id=1, source_target_pairs={{4,0},{8,4},{12,8},{16,12},{20,16},{24,20},{28,24},{32,28},{36,32}... | collective-permute-start | bytes 98312 | tf_op jit(solution)/shard_map/ppermute | solution.py:19
  17.8 1.9 collective-permute-start.1
  20.4 10.2 %select_add_fusion = f32[8,32,256]{2,1,0:T(8,128)S(1)} fusion(s32[8,32,256]{2,1,0:T(8,128)S(1)} %copy-done.114, f32[]{:T(128)} %bitcast.15, f32[]{:T(128)} %bitcast.14, f32[]{:T(128)} %bitcast.13, f32[]{:T(128)} %bitcast.12, f32[]{:T(128)} %bitcast.11, f32[]{:T(128)} %bitcast.10, f32[]{:T(128)} %bitcast.9, f32[]{:T(128)} %bitcast.8, f32[]{:T(128)} %bitcast.7, ...), kind=kLoop, calls=%fused_computation.110 | loop fusion | flops 3080192 | bytes 524352 | tf_op jit(solution)/shard_map/add | solution.py:42
  30.7 6.9 %collective-permute-start.2 = (f32[8,1,256]{2,1,0:T(1,128)S(1)}, f32[8,1,256]{2,1,0:T(1,128)S(1)}, u32[]{:S(2)}, u32[]{:S(2)}) collective-permute-start(f32[8,1,256]{2,1,0:T(1,128)S(1)} %get-tuple-element.141), channel_id=1, source_target_pairs={{4,0},{8,4},{12,8},{16,12},{20,16},{24,20},{28,24},{32,28},{36,32}... | collective-permute-start | bytes 24584 | tf_op jit(solution)/shard_map/ppermute | solution.py:19
  37.6 1.9 collective-permute-start
  39.9 1.0 broadcast_select_fusion
  40.9 5.2 %collective-permute-done = f32[8,1,256]{2,1,0:T(1,128)S(1)} collective-permute-done((f32[8,1,256]{2,1,0:T(1,128)S(1)}, f32[8,1,256]{2,1,0:T(1,128)S(1)}, u32[]{:S(2)}, u32[]{:S(2)}) %collective-permute-start) | collective-permute-done | bytes 8224 | tf_op jit(solution)/shard_map/ppermute | solution.py:17
  46.3 1.3 collective-permute-start.6
  47.6 3.0 %collective-permute-start.4 = (f32[8,34,1]{2,1,0:T(8,128)S(1)}, f32[8,34,1]{2,1,0:T(8,128)S(1)}, u32[]{:S(2)}, u32[]{:S(2)}) collective-permute-start(f32[8,34,1]{2,1,0:T(8,128)S(1)} %get-tuple-element.128), channel_id=1, source_target_pairs={{0,1},{1,2},{2,3},{4,5},{5,6},{6,7},{8,9},{9,10},{10,11},{12,13},{... | collective-permute-start | bytes 3272 | tf_op jit(solution)/shard_map/ppermute | solution.py:17
  51.3 2.8 %copy.183 = f32[4,8,32,256]{2,1,3,0:T(8,128)} copy(f32[4,8,32,256]{3,2,1,0:T(8,128)S(1)} %copy-done.3) | data formatting | bytes 2097152 | tf_op args[0]
  54.2 1.3 collective-permute-start.9
  55.5 2.7 %copy.184 = f32[4,8,1,256]{2,1,3,0:T(8,128)} copy(f32[4,8,1,256]{3,1,2,0:T(8,128)S(1)} %collective-permute-done.3) | data formatting | bytes 65536 | tf_op jit(solution)/shard_map/ppermute | solution.py:19
  58.3 2.7 %copy.182 = f32[4,8,1,256]{2,1,3,0:T(8,128)} copy(f32[4,8,1,256]{3,1,2,0:T(8,128)S(1)} %collective-permute-done.1) | data formatting | bytes 65536 | tf_op jit(solution)/shard_map/ppermute | solution.py:17
  61.0 6.9 %pad_maximum_fusion = f32[4,8,34,256]{2,1,3,0:T(8,128)S(1)} fusion(f32[4,8,1,256]{2,1,3,0:T(8,128)} %copy.184, f32[4,8,32,256]{2,1,3,0:T(8,128)} %copy.183, f32[4,8,1,256]{2,1,3,0:T(8,128)} %copy.182), kind=kLoop, calls=%fused_computation | loop fusion | flops 557056 | bytes 2228224 | tf_op jit(solution)/shard_map/concatenate | solution.py:15
  67.9 2.0 copy-done
  70.0 1.3 collective-permute-start.7
  71.2 3.2 %collective-permute-start.5 = (f32[4,8,34,1]{2,1,3,0:T(8,128)S(1)}, f32[4,8,34,1]{2,1,3,0:T(8,128)S(1)}, u32[]{:S(2)}, u32[]{:S(2)}) collective-permute-start(f32[4,8,34,1]{2,1,3,0:T(8,128)S(1)} %get-tuple-element.94), channel_id=1, source_target_pairs={{0,1},{1,2},{2,3},{4,5},{5,6},{6,7},{8,9},{9,10},{10,11},{12,13},{... | collective-permute-start | bytes 13064 | tf_op jit(solution)/shard_map/ppermute | solution.py:17
  74.5 4.6 %collective-permute-start.8 = (f32[1,34,258]{2,1,0:T(8,128)S(1)}, f32[1,34,258]{2,1,0:T(8,128)S(1)}, u32[]{:S(2)}, u32[]{:S(2)}) collective-permute-start(f32[1,34,258]{2,1,0:T(8,128)S(1)} %get-tuple-element.93), channel_id=1, source_target_pairs={{0,64},{64,128},{128,192},{1,65},{65,129},{129,193},{2,66},{66,130... | collective-permute-start | bytes 105272 | tf_op jit(solution)/shard_map/ppermute | solution.py:17
  79.4 3.0 %copy.186 = f32[4,8,34,256]{3,1,2,0:T(8,128)S(1)} copy(f32[4,8,34,256]{2,1,3,0:T(8,128)} %copy-done) | data formatting | bytes 2228224 | tf_op jit(solution)/shard_map/concatenate | solution.py:15
  82.4 1.1 copy.189
  83.5 1.2 copy.185
  88.9 1.2 fusion.69
  90.2 1.7 multiply_add_fusion.9
  94.2 0.9 copy.201
  95.1 0.9 copy.191
  96.0 2.9 %stack.22 = f32[4,8,32,256]{3,1,2,0:T(8,128)S(1)} concatenate(f32[4,1,32,256]{3,1,2,0:T(1,128)S(1)} %get-tuple-element.63, f32[4,1,32,256]{3,1,2,0:T(1,128)} %get-tuple-element.64, f32[4,1,32,256]{3,1,2,0:T(1,128)} %get-tuple-element.65, f32[4,1,32,256]{3,1,2,0:T(1,128)} %get-tuple-element.66, f32[4,1,32,256]{3,1,2,0:T(1,128)} %get-tuple-element.67, ...), dimensions={1} | concatenate | bytes 2097152 | tf_op jit(solution)/shard_map/stack | solution.py:125
  99.1 15.7 %all-gather.1 = f32[16,32,256]{2,1,0:T(8,128)S(1)} all-gather(f32[4,32,256]{2,1,0:T(8,128)S(1)} %pad_maximum_fusion.44), channel_id=3, replica_groups=mesh['gz'=4,'gx'=16,'gy'=4] {'gz'}, dimensions={0}, use_global_device_ids=true | all-gather | bytes 655360 | tf_op jit(solution)/shard_map/all_gather | solution.py:228
  115.0 3.3 %all-gather.6.cloned.1.call-done = f32[16,2,32,256]{3,2,1,0:T(8,128)} async-done(((f32[4,2,32,256]{3,2,1,0:T(8,128)}), f32[16,2,32,256]{3,2,1,0:T(8,128)}) %all-gather.6.cloned.1.call-update) | async-done | bytes 1048592 | tf_op jit(solution)/shard_map/all_gather | solution.py:229
  118.3 2.1 fusion.67
  125.9 1.0 dynamic-slice_bitcast_fusion.3
  127.6 6.2 %collective-permute-start.11 = (f32[4,8,1,256]{3,1,2,0:T(8,128)S(1)}, f32[4,8,1,256]{3,1,2,0:T(8,128)S(1)}, u32[]{:S(2)}, u32[]{:S(2)}) collective-permute-start(f32[4,8,1,256]{3,1,2,0:T(8,128)S(1)} %get-tuple-element.107), channel_id=1, source_target_pairs={{4,0},{8,4},{12,8},{16,12},{20,16},{24,20},{28,24},{32,28},{36,32}... | collective-permute-start | bytes 98312 | tf_op jit(solution)/shard_map/ppermute | solution.py:19
  133.8 1.9 collective-permute-start.10
  135.8 6.9 %collective-permute-done.10 = f32[4,8,1,256]{3,1,2,0:T(8,128)S(1)} collective-permute-done((f32[4,8,1,256]{3,1,2,0:T(8,128)S(1)}, f32[4,8,1,256]{3,1,2,0:T(8,128)S(1)}, u32[]{:S(2)}, u32[]{:S(2)}) %collective-permute-start.10) | collective-permute-done | bytes 32800 | tf_op jit(solution)/shard_map/ppermute | solution.py:17
  143.2 1.1 fusion.136
  144.4 1.4 copy.231
  145.8 1.3 collective-permute-start.13
  147.1 2.0 copy.230
  149.0 3.6 %collective-permute-start.12 = (f32[4,8,34,1]{2,1,3,0:T(8,128)}, f32[4,8,34,1]{2,1,3,0:T(8,128)}, u32[]{:S(2)}, u32[]{:S(2)}) collective-permute-start(f32[4,8,34,1]{2,1,3,0:T(8,128)} %copy.230), channel_id=1, source_target_pairs={{0,1},{1,2},{2,3},{4,5},{5,6},{6,7},{8,9},{9,10},{10,11},{12,13},{... | collective-permute-start | bytes 13064 | tf_op jit(solution)/shard_map/ppermute | solution.py:17
  152.7 1.9 copy.205
  154.5 1.9 copy.203
  156.5 2.1 pad_add_fusion
  158.8 1.2 fusion.50
  160.1 1.6 multiply_add_fusion.2
  163.1 2.5 stack.30
  165.6 19.1 %all-gather.8.cloned.1.call-done = f32[16,2,32,256]{3,2,1,0:T(8,128)} async-done(((f32[4,2,32,256]{3,2,1,0:T(8,128)}), f32[16,2,32,256]{3,2,1,0:T(8,128)}) %all-gather.8.cloned.1.call-update) | async-done | bytes 1048592 | tf_op jit(solution)/shard_map/all_gather | solution.py:229
  184.8 2.1 fusion.48
  192.3 1.0 dynamic-slice_bitcast_fusion.1
  193.4 1.4 fusion.110
  194.8 6.3 %collective-permute-start.15 = (f32[4,8,1,256]{3,1,2,0:T(8,128)S(1)}, f32[4,8,1,256]{3,1,2,0:T(8,128)S(1)}, u32[]{:S(2)}, u32[]{:S(2)}) collective-permute-start(f32[4,8,1,256]{3,1,2,0:T(8,128)S(1)} %get-tuple-element.105), channel_id=1, source_target_pairs={{4,0},{8,4},{12,8},{16,12},{20,16},{24,20},{28,24},{32,28},{36,32}... | collective-permute-start | bytes 98312 | tf_op jit(solution)/shard_map/ppermute | solution.py:19
  201.1 1.9 collective-permute-start.14
  203.0 6.9 %collective-permute-done.14 = f32[4,8,1,256]{3,1,2,0:T(8,128)S(1)} collective-permute-done((f32[4,8,1,256]{3,1,2,0:T(8,128)S(1)}, f32[4,8,1,256]{3,1,2,0:T(8,128)S(1)}, u32[]{:S(2)}, u32[]{:S(2)}) %collective-permute-start.14) | collective-permute-done | bytes 32800 | tf_op jit(solution)/shard_map/ppermute | solution.py:17
  210.0 1.1 fusion.135
  211.2 1.4 copy.241
  212.5 1.3 collective-permute-start.17
  213.8 1.4 copy.240
  215.2 3.0 %collective-permute-start.16 = (f32[4,8,34,1]{2,1,3,0:T(8,128)S(1)}, f32[4,8,34,1]{2,1,3,0:T(8,128)S(1)}, u32[]{:S(2)}, u32[]{:S(2)}) collective-permute-start(f32[4,8,34,1]{2,1,3,0:T(8,128)S(1)} %copy.240), channel_id=1, source_target_pairs={{0,1},{1,2},{2,3},{4,5},{5,6},{6,7},{8,9},{9,10},{10,11},{12,13},{... | collective-permute-start | bytes 13064 | tf_op jit(solution)/shard_map/ppermute | solution.py:17
  218.2 1.3 copy.221
  219.5 1.2 copy.219
  220.7 1.1 copy.217
  221.8 1.9 fusion.2
  223.8 8.2 %copy.220 = f32[4,8,32,256]{1,3,2,0:T(8,128)} copy(f32[4,8,32,256]{3,1,2,0:T(8,128)S(1)} %fusion.2) | data formatting | bytes 2097152 | tf_op jit(solution)/shard_map/add | solution.py:65
  232.0 17.5 %reduce_sum.9 = f32[4,8,16,128]{1,3,2,0:T(8,128)} reduce(f32[4,8,16,2,128,2]{1,5,4,3,2,0:T(2,128)} %bitcast.376, f32[]{:T(128)} %constant.36.clone.1), dimensions={3,5}, to_apply=%region_0.1 | reduce | flops 196608 | bytes 1310724 | tf_op jit(solution)/shard_map/reduce_sum | solution.py:246
  249.5 3.5 %copy.222 = f32[4,8,16,128]{3,2,1,0:T(8,128)} copy(f32[4,8,16,128]{1,3,2,0:T(8,128)} %reduce_sum.9) | data formatting | bytes 524288
  (343 shorter events, 22.3 us)
Async XLA Ops:
  7.2 12.5 %copy-start.122 = (f32[16]{0:T(128)S(1)}, f32[16]{0:T(128)}, u32[]{:S(2)}) copy-start(f32[16]{0:T(128)} %param.6) | copy-start | bytes 196
  7.2 13.2 %copy-start.114 = (s32[8,32,256]{2,1,0:T(8,128)S(1)}, s32[8,32,256]{2,1,0:T(8,128)}, u32[]{:S(2)}) copy-start(s32[8,32,256]{2,1,0:T(8,128)} %param.5) | copy-start | bytes 786436
  7.2 32.4 %copy-start.123 = (s32[4,4]{1,0:T(4,128)S(1)}, s32[4,4]{1,0:T(4,128)}, u32[]{:S(2)}) copy-start(s32[4,4]{1,0:T(4,128)} %param.7) | copy-start | bytes 196
  7.2 111.1 %all-gather.6.cloned.1.call-start = ((), (), s32[]{:S(2)}) async-start(), calls=%async_computation | async-start | bytes 1310720 | tf_op jit(solution)/shard_map/all_gather | solution.py:229
  9.1 42.2 %copy-start.3 = (f32[4,8,32,256]{3,2,1,0:T(8,128)S(1)}, f32[4,8,32,256]{3,2,1,0:T(8,128)}, u32[]{:S(2)}) copy-start(f32[4,8,32,256]{3,2,1,0:T(8,128)} %param.4) | copy-start | bytes 3145732
  9.1 46.4 %collective-permute-start.3 = (f32[4,8,1,256]{3,1,2,0:T(8,128)S(1)}, f32[4,8,1,256]{3,1,2,0:T(8,128)S(1)}, u32[]{:S(2)}, u32[]{:S(2)}) collective-permute-start(f32[4,8,1,256]{3,1,2,0:T(8,128)S(1)} %get-tuple-element.109), channel_id=1, source_target_pairs={{4,0},{8,4},{12,8},{16,12},{20,16},{24,20},{28,24},{32,28},{36,32}... | collective-permute-start | bytes 98312 | tf_op jit(solution)/shard_map/ppermute | solution.py:19
  17.8 40.5 %collective-permute-start.1 = (f32[4,8,1,256]{3,1,2,0:T(8,128)S(1)}, f32[4,8,1,256]{3,1,2,0:T(8,128)S(1)}, u32[]{:S(2)}, u32[]{:S(2)}) collective-permute-start(f32[4,8,1,256]{3,1,2,0:T(8,128)S(1)} %get-tuple-element.108), channel_id=1, source_target_pairs={{0,4},{4,8},{8,12},{12,16},{16,20},{20,24},{24,28},{28,32},{32,36}... | collective-permute-start | bytes 98312 | tf_op jit(solution)/shard_map/ppermute | solution.py:17
  30.7 10.3 %collective-permute-start.2 = (f32[8,1,256]{2,1,0:T(1,128)S(1)}, f32[8,1,256]{2,1,0:T(1,128)S(1)}, u32[]{:S(2)}, u32[]{:S(2)}) collective-permute-start(f32[8,1,256]{2,1,0:T(1,128)S(1)} %get-tuple-element.141), channel_id=1, source_target_pairs={{4,0},{8,4},{12,8},{16,12},{20,16},{24,20},{28,24},{32,28},{36,32}... | collective-permute-start | bytes 24584 | tf_op jit(solution)/shard_map/ppermute | solution.py:19
  37.6 8.6 %collective-permute-start = (f32[8,1,256]{2,1,0:T(1,128)S(1)}, f32[8,1,256]{2,1,0:T(1,128)S(1)}, u32[]{:S(2)}, u32[]{:S(2)}) collective-permute-start(f32[8,1,256]{2,1,0:T(1,128)S(1)} %get-tuple-element.140), channel_id=1, source_target_pairs={{0,4},{4,8},{8,12},{12,16},{16,20},{20,24},{24,28},{28,32},{32,36}... | collective-permute-start | bytes 24584 | tf_op jit(solution)/shard_map/ppermute | solution.py:17
  46.3 7.8 %collective-permute-start.6 = (f32[8,34,1]{2,1,0:T(8,128)S(1)}, f32[8,34,1]{2,1,0:T(8,128)S(1)}, u32[]{:S(2)}, u32[]{:S(2)}) collective-permute-start(f32[8,34,1]{2,1,0:T(8,128)S(1)} %get-tuple-element.129), channel_id=1, source_target_pairs={{1,0},{2,1},{3,2},{5,4},{6,5},{7,6},{9,8},{10,9},{11,10},{13,12},{... | collective-permute-start | bytes 3272 | tf_op jit(solution)/shard_map/ppermute | solution.py:19
  47.6 6.5 %collective-permute-start.4 = (f32[8,34,1]{2,1,0:T(8,128)S(1)}, f32[8,34,1]{2,1,0:T(8,128)S(1)}, u32[]{:S(2)}, u32[]{:S(2)}) collective-permute-start(f32[8,34,1]{2,1,0:T(8,128)S(1)} %get-tuple-element.128), channel_id=1, source_target_pairs={{0,1},{1,2},{2,3},{4,5},{5,6},{6,7},{8,9},{9,10},{10,11},{12,13},{... | collective-permute-start | bytes 3272 | tf_op jit(solution)/shard_map/ppermute | solution.py:17
  54.1 30.6 %copy-start.6 = (f32[8,34,1]{2,1,0:T(8,128)}, f32[8,34,1]{2,1,0:T(8,128)S(1)}, u32[]{:S(2)}) copy-start(f32[8,34,1]{2,1,0:T(8,128)S(1)} %collective-permute-done.6) | copy-start | bytes 3268
  54.1 30.6 %copy-start.8 = (f32[8,34,1]{2,1,0:T(8,128)}, f32[8,34,1]{2,1,0:T(8,128)S(1)}, u32[]{:S(2)}) copy-start(f32[8,34,1]{2,1,0:T(8,128)S(1)} %collective-permute-done.4) | copy-start | bytes 3268
  54.2 20.2 %collective-permute-start.9 = (f32[1,34,258]{2,1,0:T(8,128)S(1)}, f32[1,34,258]{2,1,0:T(8,128)S(1)}, u32[]{:S(2)}, u32[]{:S(2)}) collective-permute-start(f32[1,34,258]{2,1,0:T(8,128)S(1)} %pad_maximum_fusion.46), channel_id=1, source_target_pairs={{64,0},{128,64},{192,128},{65,1},{129,65},{193,129},{66,2},{130,66... | collective-permute-start | bytes 105272 | tf_op jit(solution)/shard_map/ppermute | solution.py:19
  70.0 12.4 %collective-permute-start.7 = (f32[4,8,34,1]{2,1,3,0:T(8,128)S(1)}, f32[4,8,34,1]{2,1,3,0:T(8,128)S(1)}, u32[]{:S(2)}, u32[]{:S(2)}) collective-permute-start(f32[4,8,34,1]{2,1,3,0:T(8,128)S(1)} %get-tuple-element.95), channel_id=1, source_target_pairs={{1,0},{2,1},{3,2},{5,4},{6,5},{7,6},{9,8},{10,9},{11,10},{13,12},{... | collective-permute-start | bytes 13064 | tf_op jit(solution)/shard_map/ppermute | solution.py:19
  71.2 12.3 %collective-permute-start.5 = (f32[4,8,34,1]{2,1,3,0:T(8,128)S(1)}, f32[4,8,34,1]{2,1,3,0:T(8,128)S(1)}, u32[]{:S(2)}, u32[]{:S(2)}) collective-permute-start(f32[4,8,34,1]{2,1,3,0:T(8,128)S(1)} %get-tuple-element.94), channel_id=1, source_target_pairs={{0,1},{1,2},{2,3},{4,5},{5,6},{6,7},{8,9},{9,10},{10,11},{12,13},{... | collective-permute-start | bytes 13064 | tf_op jit(solution)/shard_map/ppermute | solution.py:17
  74.5 10.2 %collective-permute-start.8 = (f32[1,34,258]{2,1,0:T(8,128)S(1)}, f32[1,34,258]{2,1,0:T(8,128)S(1)}, u32[]{:S(2)}, u32[]{:S(2)}) collective-permute-start(f32[1,34,258]{2,1,0:T(8,128)S(1)} %get-tuple-element.93), channel_id=1, source_target_pairs={{0,64},{64,128},{128,192},{1,65},{65,129},{129,193},{2,66},{66,130... | collective-permute-start | bytes 105272 | tf_op jit(solution)/shard_map/ppermute | solution.py:17
  79.4 5.3 %copy-start.124 = (pred[8]{0:T(512)(128)(4,1)S(1)}, pred[8]{0:T(512)(128)(4,1)}, u32[]{:S(2)}) copy-start(pred[8]{0:T(512)(128)(4,1)} %constant.81.clone.1) | copy-start | bytes 28
  92.9 91.9 %all-gather.8.cloned.1.call-start = ((), (), s32[]{:S(2)}) async-start(), calls=%async_computation.1 | async-start | bytes 1310720 | tf_op jit(solution)/shard_map/all_gather | solution.py:229
  95.1 3.8 %copy-start.70 = (f32[32,256]{1,0:T(8,128)S(1)}, f32[32,256]{1,0:T(8,128)}, u32[]{:S(2)}) copy-start(f32[32,256]{1,0:T(8,128)} %copy-done.68) | copy-start | bytes 98308
  95.1 3.8 %copy-start.74 = (f32[32,256]{1,0:T(8,128)S(1)}, f32[32,256]{1,0:T(8,128)}, u32[]{:S(2)}) copy-start(f32[32,256]{1,0:T(8,128)} %copy-done.72) | copy-start | bytes 98308
  95.1 3.8 %copy-start.78 = (f32[32,256]{1,0:T(8,128)S(1)}, f32[32,256]{1,0:T(8,128)}, u32[]{:S(2)}) copy-start(f32[32,256]{1,0:T(8,128)} %copy-done.76) | copy-start | bytes 98308
  114.8 5.6 %copy-start.93 = (f32[32,256]{1,0:T(8,128)}, f32[32,256]{1,0:T(8,128)S(1)}, u32[]{:S(2)}) copy-start(f32[32,256]{1,0:T(8,128)S(1)} %get-tuple-element.48) | copy-start | bytes 98308
  114.8 5.6 %copy-start.95 = (f32[32,256]{1,0:T(8,128)}, f32[32,256]{1,0:T(8,128)S(1)}, u32[]{:S(2)}) copy-start(f32[32,256]{1,0:T(8,128)S(1)} %get-tuple-element.50) | copy-start | bytes 98308
  114.8 5.6 %copy-start.97 = (f32[32,256]{1,0:T(8,128)}, f32[32,256]{1,0:T(8,128)S(1)}, u32[]{:S(2)}) copy-start(f32[32,256]{1,0:T(8,128)S(1)} %get-tuple-element.51) | copy-start | bytes 98308
  114.8 7.0 %copy-start.89 = (f32[32,256]{1,0:T(8,128)}, f32[32,256]{1,0:T(8,128)S(1)}, u32[]{:S(2)}) copy-start(f32[32,256]{1,0:T(8,128)S(1)} %get-tuple-element.49) | copy-start | bytes 98308
  114.9 8.3 %copy-start.91 = (f32[32,256]{1,0:T(8,128)}, f32[32,256]{1,0:T(8,128)S(1)}, u32[]{:S(2)}) copy-start(f32[32,256]{1,0:T(8,128)S(1)} %get-tuple-element.47) | copy-start | bytes 98308
  114.9 9.7 %copy-start.106 = (f32[32,256]{1,0:T(8,128)}, f32[32,256]{1,0:T(8,128)S(1)}, u32[]{:S(2)}) copy-start(f32[32,256]{1,0:T(8,128)S(1)} %get-tuple-element.46) | copy-start | bytes 98308
  114.9 5.5 %copy-start.105 = (f32[32,256]{1,0:T(8,128)}, f32[32,256]{1,0:T(8,128)S(1)}, u32[]{:S(2)}) copy-start(f32[32,256]{1,0:T(8,128)S(1)} %get-tuple-element.123) | copy-start | bytes 98308
  114.9 9.0 %copy-start.19 = (f32[32,256]{1,0:T(8,128)}, f32[32,256]{1,0:T(8,128)S(1)}, u32[]{:S(2)}) copy-start(f32[32,256]{1,0:T(8,128)S(1)} %get-tuple-element.122) | copy-start | bytes 98308
  114.9 6.9 %copy-start.98 = (f32[32,256]{1,0:T(8,128)}, f32[32,256]{1,0:T(8,128)S(1)}, u32[]{:S(2)}) copy-start(f32[32,256]{1,0:T(8,128)S(1)} %get-tuple-element.113) | copy-start | bytes 98308
  115.0 6.8 %copy-start.99 = (f32[32,256]{1,0:T(8,128)}, f32[32,256]{1,0:T(8,128)S(1)}, u32[]{:S(2)}) copy-start(f32[32,256]{1,0:T(8,128)S(1)} %get-tuple-element.115) | copy-start | bytes 98308
  115.0 6.8 %copy-start.100 = (f32[32,256]{1,0:T(8,128)}, f32[32,256]{1,0:T(8,128)S(1)}, u32[]{:S(2)}) copy-start(f32[32,256]{1,0:T(8,128)S(1)} %get-tuple-element.117) | copy-start | bytes 98308
  115.0 6.8 %copy-start.101 = (f32[32,256]{1,0:T(8,128)}, f32[32,256]{1,0:T(8,128)S(1)}, u32[]{:S(2)}) copy-start(f32[32,256]{1,0:T(8,128)S(1)} %get-tuple-element.118) | copy-start | bytes 98308
  115.0 6.8 %copy-start.102 = (f32[32,256]{1,0:T(8,128)}, f32[32,256]{1,0:T(8,128)S(1)}, u32[]{:S(2)}) copy-start(f32[32,256]{1,0:T(8,128)S(1)} %get-tuple-element.119) | copy-start | bytes 98308
  115.0 6.8 %copy-start.103 = (f32[32,256]{1,0:T(8,128)}, f32[32,256]{1,0:T(8,128)S(1)}, u32[]{:S(2)}) copy-start(f32[32,256]{1,0:T(8,128)S(1)} %get-tuple-element.120) | copy-start | bytes 98308
  115.0 6.8 %copy-start.104 = (f32[32,256]{1,0:T(8,128)}, f32[32,256]{1,0:T(8,128)S(1)}, u32[]{:S(2)}) copy-start(f32[32,256]{1,0:T(8,128)S(1)} %get-tuple-element.121) | copy-start | bytes 98308
  115.0 6.8 %copy-start.110 = (f32[32,256]{1,0:T(8,128)}, f32[32,256]{1,0:T(8,128)S(1)}, u32[]{:S(2)}) copy-start(f32[32,256]{1,0:T(8,128)S(1)} %get-tuple-element.116) | copy-start | bytes 98308
  115.0 9.5 %copy-start.108 = (f32[32,256]{1,0:T(8,128)}, f32[32,256]{1,0:T(8,128)S(1)}, u32[]{:S(2)}) copy-start(f32[32,256]{1,0:T(8,128)S(1)} %get-tuple-element.112) | copy-start | bytes 98308
  122.5 4.4 %copy-start.12 = (f32[8,32,256]{2,0,1:T(8,128)S(1)}, f32[8,32,256]{2,0,1:T(8,128)}, u32[]{:S(2)}) copy-start(f32[8,32,256]{2,0,1:T(8,128)} %copy.201) | copy-start | bytes 786436
  122.5 4.4 %copy-start.13 = (f32[8,32,256]{2,0,1:T(8,128)S(1)}, f32[8,32,256]{2,0,1:T(8,128)}, u32[]{:S(2)}) copy-start(f32[8,32,256]{2,0,1:T(8,128)} %copy.191) | copy-start | bytes 786436
  127.6 8.1 %collective-permute-start.11 = (f32[4,8,1,256]{3,1,2,0:T(8,128)S(1)}, f32[4,8,1,256]{3,1,2,0:T(8,128)S(1)}, u32[]{:S(2)}, u32[]{:S(2)}) collective-permute-start(f32[4,8,1,256]{3,1,2,0:T(8,128)S(1)} %get-tuple-element.107), channel_id=1, source_target_pairs={{4,0},{8,4},{12,8},{16,12},{20,16},{24,20},{28,24},{32,28},{36,32}... | collective-permute-start | bytes 98312 | tf_op jit(solution)/shard_map/ppermute | solution.py:19
  133.8 8.8 %collective-permute-start.10 = (f32[4,8,1,256]{3,1,2,0:T(8,128)S(1)}, f32[4,8,1,256]{3,1,2,0:T(8,128)S(1)}, u32[]{:S(2)}, u32[]{:S(2)}) collective-permute-start(f32[4,8,1,256]{3,1,2,0:T(8,128)S(1)} %get-tuple-element.106), channel_id=1, source_target_pairs={{0,4},{4,8},{8,12},{12,16},{16,20},{20,24},{24,28},{28,32},{32,36}... | collective-permute-start | bytes 98312 | tf_op jit(solution)/shard_map/ppermute | solution.py:17
  135.7 7.0 %copy-start.119 = (f32[4,8,1,256]{3,1,2,0:T(8,128)}, f32[4,8,1,256]{3,1,2,0:T(8,128)S(1)}, u32[]{:S(2)}) copy-start(f32[4,8,1,256]{3,1,2,0:T(8,128)S(1)} %collective-permute-done.11) | copy-start | bytes 98308
  144.4 12.0 %copy-start.2 = (f32[8,32,256]{2,0,1:T(8,128)S(1)}, f32[8,32,256]{2,0,1:T(8,128)}, u32[]{:S(2)}) copy-start(f32[8,32,256]{2,0,1:T(8,128)} %copy-done.1) | copy-start | bytes 786436
  145.8 6.9 %collective-permute-start.13 = (f32[4,8,34,1]{2,1,3,0:T(8,128)S(1)}, f32[4,8,34,1]{2,1,3,0:T(8,128)}, u32[]{:S(2)}, u32[]{:S(2)}) collective-permute-start(f32[4,8,34,1]{2,1,3,0:T(8,128)S(1)} %copy.231), channel_id=1, source_target_pairs={{1,0},{2,1},{3,2},{5,4},{6,5},{7,6},{9,8},{10,9},{11,10},{13,12},{... | collective-permute-start | bytes 13064 | tf_op jit(solution)/shard_map/ppermute | solution.py:19
  149.0 5.5 %collective-permute-start.12 = (f32[4,8,34,1]{2,1,3,0:T(8,128)}, f32[4,8,34,1]{2,1,3,0:T(8,128)}, u32[]{:S(2)}, u32[]{:S(2)}) collective-permute-start(f32[4,8,34,1]{2,1,3,0:T(8,128)} %copy.230), channel_id=1, source_target_pairs={{0,1},{1,2},{2,3},{4,5},{5,6},{6,7},{8,9},{9,10},{10,11},{12,13},{... | collective-permute-start | bytes 13064 | tf_op jit(solution)/shard_map/ppermute | solution.py:17
  162.4 22.4 %copy-start.20 = (f32[32,256]{1,0:T(8,128)S(1)}, f32[32,256]{1,0:T(8,128)}, u32[]{:S(2)}) copy-start(f32[32,256]{1,0:T(8,128)} %copy-done.19) | copy-start | bytes 98308
  162.4 22.4 %copy-start.94 = (f32[32,256]{1,0:T(8,128)S(1)}, f32[32,256]{1,0:T(8,128)}, u32[]{:S(2)}) copy-start(f32[32,256]{1,0:T(8,128)} %copy-done.93) | copy-start | bytes 98308
  162.4 22.4 %copy-start.96 = (f32[32,256]{1,0:T(8,128)S(1)}, f32[32,256]{1,0:T(8,128)}, u32[]{:S(2)}) copy-start(f32[32,256]{1,0:T(8,128)} %copy-done.95) | copy-start | bytes 98308
  165.6 21.3 %copy-start.111 = (f32[32,256]{1,0:T(8,128)S(1)}, f32[32,256]{1,0:T(8,128)}, u32[]{:S(2)}) copy-start(f32[32,256]{1,0:T(8,128)} %copy-done.110) | copy-start | bytes 98308
  184.8 3.5 %copy-start.90 = (f32[32,256]{1,0:T(8,128)S(1)}, f32[32,256]{1,0:T(8,128)}, u32[]{:S(2)}) copy-start(f32[32,256]{1,0:T(8,128)} %copy-done.89) | copy-start | bytes 98308
  184.8 4.8 %copy-start.92 = (f32[32,256]{1,0:T(8,128)S(1)}, f32[32,256]{1,0:T(8,128)}, u32[]{:S(2)}) copy-start(f32[32,256]{1,0:T(8,128)} %copy-done.91) | copy-start | bytes 98308
  186.9 4.1 %copy-start.107 = (f32[32,256]{1,0:T(8,128)S(1)}, f32[32,256]{1,0:T(8,128)}, u32[]{:S(2)}) copy-start(f32[32,256]{1,0:T(8,128)} %copy-done.106) | copy-start | bytes 98308
  186.9 4.1 %copy-start.109 = (f32[32,256]{1,0:T(8,128)S(1)}, f32[32,256]{1,0:T(8,128)}, u32[]{:S(2)}) copy-start(f32[32,256]{1,0:T(8,128)} %copy-done.108) | copy-start | bytes 98308
  189.0 4.4 %copy-start.4 = (f32[4,8,32,256]{3,1,2,0:T(8,128)S(1)}, f32[4,8,32,256]{3,1,2,0:T(8,128)}, u32[]{:S(2)}) copy-start(f32[4,8,32,256]{3,1,2,0:T(8,128)} %stack.30) | copy-start | bytes 3145732
  189.0 4.4 %copy-start.14 = (f32[8,32,256]{2,0,1:T(8,128)S(1)}, f32[8,32,256]{2,0,1:T(8,128)}, u32[]{:S(2)}) copy-start(f32[8,32,256]{2,0,1:T(8,128)} %copy.191) | copy-start | bytes 786436
  189.0 4.4 %copy-start.59 = (f32[4,32,256]{2,1,0:T(8,128)S(1)}, f32[4,32,256]{2,1,0:T(8,128)}, u32[]{:S(2)}) copy-start(f32[4,32,256]{2,1,0:T(8,128)} %copy-done.58) | copy-start | bytes 393220
  189.0 4.4 %copy-start.61 = (f32[4,32,256]{2,1,0:T(8,128)S(1)}, f32[4,32,256]{2,1,0:T(8,128)}, u32[]{:S(2)}) copy-start(f32[4,32,256]{2,1,0:T(8,128)} %copy-done.60) | copy-start | bytes 393220
  194.8 8.2 %collective-permute-start.15 = (f32[4,8,1,256]{3,1,2,0:T(8,128)S(1)}, f32[4,8,1,256]{3,1,2,0:T(8,128)S(1)}, u32[]{:S(2)}, u32[]{:S(2)}) collective-permute-start(f32[4,8,1,256]{3,1,2,0:T(8,128)S(1)} %get-tuple-element.105), channel_id=1, source_target_pairs={{4,0},{8,4},{12,8},{16,12},{20,16},{24,20},{28,24},{32,28},{36,32}... | collective-permute-start | bytes 98312 | tf_op jit(solution)/shard_map/ppermute | solution.py:19
  201.1 8.8 %collective-permute-start.14 = (f32[4,8,1,256]{3,1,2,0:T(8,128)S(1)}, f32[4,8,1,256]{3,1,2,0:T(8,128)S(1)}, u32[]{:S(2)}, u32[]{:S(2)}) collective-permute-start(f32[4,8,1,256]{3,1,2,0:T(8,128)S(1)} %get-tuple-element.104), channel_id=1, source_target_pairs={{0,4},{4,8},{8,12},{12,16},{16,20},{20,24},{24,28},{28,32},{32,36}... | collective-permute-start | bytes 98312 | tf_op jit(solution)/shard_map/ppermute | solution.py:17
  210.0 8.2 %copy-start.5 = (f32[4,8,32,256]{3,1,2,0:T(8,128)S(1)}, f32[4,8,32,256]{3,1,2,0:T(8,128)}, u32[]{:S(2)}) copy-start(f32[4,8,32,256]{3,1,2,0:T(8,128)} %get-tuple-element.13) | copy-start | bytes 3145732
  212.5 7.0 %collective-permute-start.17 = (f32[4,8,34,1]{2,1,3,0:T(8,128)S(1)}, f32[4,8,34,1]{2,1,3,0:T(8,128)S(1)}, u32[]{:S(2)}, u32[]{:S(2)}) collective-permute-start(f32[4,8,34,1]{2,1,3,0:T(8,128)S(1)} %copy.241), channel_id=1, source_target_pairs={{1,0},{2,1},{3,2},{5,4},{6,5},{7,6},{9,8},{10,9},{11,10},{13,12},{... | collective-permute-start | bytes 13064 | tf_op jit(solution)/shard_map/ppermute | solution.py:19
  215.2 5.5 %collective-permute-start.16 = (f32[4,8,34,1]{2,1,3,0:T(8,128)S(1)}, f32[4,8,34,1]{2,1,3,0:T(8,128)S(1)}, u32[]{:S(2)}, u32[]{:S(2)}) collective-permute-start(f32[4,8,34,1]{2,1,3,0:T(8,128)S(1)} %copy.240), channel_id=1, source_target_pairs={{0,1},{1,2},{2,3},{4,5},{5,6},{6,7},{8,9},{9,10},{10,11},{12,13},{... | collective-permute-start | bytes 13064 | tf_op jit(solution)/shard_map/ppermute | solution.py:17
  (81 other events, 137.3 us)
Sparse Core Ops, SparseCore 0:
  93.0 25.2 all-gather.5
  162.6 22.1 all-gather.7
where the time goes:
time: 262 us; the launch traced here: 260 us
  other arithmetic  63.6 us (24%)
  local copies, waits for them, and re-layouts  63.4 us (24%)
  starting transfers between devices  59.6 us (23%)
  waiting for transfers between devices  41.4 us (16%)
  between operations  16.1 us (6%)
  blocking collectives  15.7 us (6%)
    ppermute x9, starting transfers between devices, with_halo(): lax.ppermute(head, axis, [((i + 1) % count, i) for i in range(ends)])  34.4 us
    ppermute x9, starting transfers between devices, with_halo(): lax.ppermute(tail, axis, [(i, (i + 1) % count) for i in range(ends)])  25.1 us
    unnamed x267, local copies, waits for them, and re-layouts  23.8 us
    all_gather x2, waiting for transfers between devices, relax(): lax.all_gather(value_ends(local_part), 'gz', axis=0, tiled=True)  22.4 us
    ppermute x9, waiting for transfers between devices, with_halo(): lax.ppermute(tail, axis, [(i, (i + 1) % count) for i in range(ends)])  19 us
    reduce_sum x1, other arithmetic, body(): coarse_residual = defect.reshape(source_count, depth_cells, width_x // 2,...  17.5 us
    all_gather x1, blocking collectives, relax(): lax.all_gather(spread_ends(spreads), 'gz', axis=0, tiled=True)  15.7 us
    unnamed x16, other arithmetic  11.1 us
  transfers between devices with their start and end apart: 20, of which 5 were waited for; matrix products, arithmetic and copies ran while one was open for 19% of the time, Pallas kernels for 0%

commit v1 on v0

v1 whole, which is shorter than its diff:
```python
import functools

import jax
import jax.numpy as jnp
from jax import lax
from jax.experimental import pallas as pl
from jax.experimental.pallas import tpu as pltpu
from jax.sharding import PartitionSpec as P

ASPECT = 128
MESH = pl.DeviceIdType.MESH
F32 = jnp.float32
UNROLL = False


def roll(v, shift, axis):
    return pltpu.roll(v, shift, axis)


def recip(v):
    return pltpu.reciprocal(v, approx=True)


def loop(count, body, init):
    if UNROLL:
        for i in range(count):
            init = body(i, init)
        return init
    return lax.fori_loop(0, count, body, init)


def kernel(
    nz, nx, ny,
    pot, lab, cond, elec, out, coarse,
    p_nat, l_nat, sg, xp, xh, yp, yh, src,
    lw_r, le_r, ls_r, ln_r, inv_r, e_r, rt_r, g_r, r_r, ss,
    fw, fp, ch, on, df, co, ends, wab, km, tt,
    m1s, m1r, m2s, m2r, m3s, m3r,
    loc, zs, zr, xs, xr, ys, yr, ms, mr,
):
    p = lax.axis_index("gz")
    gx = lax.axis_index("gx")
    gy = lax.axis_index("gy")
    has_w, has_e = gx > 0, gx < nx - 1
    has_u, has_d = p > 0, p < nz - 1
    up = p < nz // 2
    is_end = (p == 0) | (p == nz - 1)
    is_mid = (p > 0) & (p < nz - 1)
    west, east = {"gx": gx - 1}, {"gx": gx + 1}
    south, north = {"gy": lax.rem(gy + ny - 1, ny)}, {"gy": lax.rem(gy + 1, ny)}
    above, below = {"gz": p - 1}, {"gz": p + 1}
    lane = lax.broadcasted_iota(jnp.int32, (16, 128), 1)
    lane32 = lax.broadcasted_iota(jnp.int32, (32, 128), 1)
    sub8 = lax.broadcasted_iota(jnp.int32, (8, 128), 0)
    row16 = lax.broadcasted_iota(jnp.int32, (16, 128), 0)

    lab_cp = [
        pltpu.make_async_copy(lab.at[:, :, c * 128:(c + 1) * 128], l_nat.at[:, c], loc.at[0, c])
        for c in range(2)
    ]
    pot_cp = [
        pltpu.make_async_copy(pot.at[:, :, :, c * 128:(c + 1) * 128], p_nat.at[:, :, c], loc.at[1, c])
        for c in range(2)
    ]
    for cp in lab_cp + pot_cp:
        cp.start()

    @pl.when(gx == 0)
    def _():
        xh[:, 0] = jnp.zeros((3, 2, 40, 128), F32)

    @pl.when(gx == nx - 1)
    def _():
        xh[:, 1] = jnp.zeros((3, 2, 40, 128), F32)

    barrier = pltpu.get_barrier_semaphore()

    def greet(device):
        pl.semaphore_signal(barrier, inc=1, device_id=device, device_id_type=MESH)

    greet(south)
    greet(north)
    for cond_here, device in ((has_w, west), (has_e, east), (has_u, above), (has_d, below)):
        pl.when(cond_here)(functools.partial(greet, device))

    for cp in lab_cp:
        cp.wait()
    table = [cond[i] for i in range(16)]

    def lookup(z, carry):
        for c in range(2):
            l = jnp.concatenate([l_nat[z, c, pl.ds(j, 8, stride=4), :] for j in range(4)], 0)
            level = table
            for bit in range(4):
                on_bit = (l & (1 << bit)) != 0
                level = [
                    jnp.where(on_bit, level[2 * i + 1], level[2 * i]) for i in range(len(level) // 2)
                ]
            sg[z + 1, c] = recip(level[0])
        return carry

    loop(8, lookup, 0)

    @pl.when(p == 0)
    def _():
        sg[0] = sg[1]

    @pl.when(p == nz - 1)
    def _():
        sg[9] = sg[8]

    pl.semaphore_wait(
        barrier,
        2 + has_w.astype(jnp.int32) + has_e.astype(jnp.int32)
        + has_u.astype(jnp.int32) + has_d.astype(jnp.int32),
    )

    def remote(src_ref, dst_ref, send, recv, device):
        return pltpu.make_async_remote_copy(
            src_ref=src_ref, dst_ref=dst_ref, send_sem=send, recv_sem=recv,
            device_id=device, device_id_type=MESH,
        )

    to_above = remote(sg.at[1], sg.at[9], zs.at[0], zr.at[1], above)
    to_below = remote(sg.at[8], sg.at[0], zs.at[1], zr.at[0], below)
    pl.when(has_u)(to_above.start)
    pl.when(has_d)(to_below.start)

    def lateral_copies(t):
        n = 40 if t == 0 else 32
        return (
            remote(xp.at[t, 0, :, 0:n], xh.at[t, 1, :, 0:n], xs.at[t, 0], xr.at[t, 1], west),
            remote(xp.at[t, 1, :, 0:n], xh.at[t, 0, :, 0:n], xs.at[t, 1], xr.at[t, 0], east),
            remote(yp.at[t, 0], yh.at[t, 1], ys.at[t, 0], yr.at[t, 1], south),
            remote(yp.at[t, 1], yh.at[t, 0], ys.at[t, 1], yr.at[t, 0], north),
        )

    lat = [lateral_copies(t) for t in range(3)]

    def send_x(t):
        pl.when(has_w)(lat[t][0].start)
        pl.when(has_e)(lat[t][1].start)

    def send_y(t):
        lat[t][2].start()
        lat[t][3].start()

    def wait_x(t):
        pl.when(has_e)(lat[t][0].wait_recv)
        pl.when(has_w)(lat[t][1].wait_recv)

    def wait_y(t):
        lat[t][2].wait_recv()
        lat[t][3].wait_recv()

    def pack_sigma(z, acc):
        acc_s, acc_n = acc
        v0, v1 = sg[z + 1, 0], sg[z + 1, 1]
        acc_s = jnp.where(lane32 == 32 + z, roll(v0, 32 + z, 1), acc_s)
        acc_n = jnp.where(lane32 == 32 + z, roll(v1, 33 + z, 1), acc_n)
        for c, v in ((0, v0), (1, v1)):
            xp[0, 0, c, pl.ds(32 + z, 1), :] = v[0:1]
            xp[0, 1, c, pl.ds(32 + z, 1), :] = v[31:32]
        return acc_s, acc_n

    zero32 = jnp.zeros((32, 128), F32)
    acc = loop(8, pack_sigma, (zero32, zero32))
    for cp in pot_cp:
        cp.wait()

    def pack_pot(z, acc):
        acc_s, acc_n = acc
        for s in range(4):
            k = s * 8 + z
            v0, v1 = (
                jnp.concatenate([p_nat[s, z, c, pl.ds(j, 8, stride=4), :] for j in range(4)], 0)
                for c in range(2)
            )
            acc_s = jnp.where(lane32 == k, roll(v0, k, 1), acc_s)
            acc_n = jnp.where(lane32 == k, roll(v1, k + 1, 1), acc_n)
            for c in range(2):
                xp[0, 0, c, pl.ds(k, 1), :] = p_nat[s, z, c, 0:1, :]
                xp[0, 1, c, pl.ds(k, 1), :] = p_nat[s, z, c, 31:32, :]
        return acc_s, acc_n

    acc = loop(8, pack_pot, acc)
    send_x(0)
    yp[0, 0], yp[0, 1] = acc
    send_y(0)

    here = jnp.where(p == 0, 4.0 * ASPECT, 0.0).astype(F32)
    row32 = lax.broadcasted_iota(jnp.int32, (32, 128), 0)
    x_cell = gx * 32 + 4 * (row32 % 8) + row32 // 8
    for c in range(2):
        y_cell = gy * 256 + c * 128 + lane32
        for s in range(4):
            first = jnp.where((x_cell == elec[s, 0]) & (y_cell == elec[s, 1]), here, 0.0)
            second = jnp.where((x_cell == elec[s, 2]) & (y_cell == elec[s, 3]), here, 0.0)
            src[s, c] = first - second

    def centre(g, v):
        return v[8:24] if g == 0 else jnp.concatenate([v[0:8], v[24:32]], 0)

    def west_east(g, v, halo_w, halo_e):
        if g == 0:
            return v[0:16], v[16:32]
        w0 = jnp.where(sub8 == 0, halo_w(), roll(v[24:32], 1, 0))
        e3 = jnp.where(sub8 == 7, halo_e(), roll(v[0:8], 7, 0))
        return jnp.concatenate([w0, v[16:24]], 0), jnp.concatenate([v[8:16], e3], 0)

    def south_north(v0, v1, halo_s, halo_n):
        r0, r1, q0, q1 = roll(v0, 1, 1), roll(v1, 1, 1), roll(v0, 127, 1), roll(v1, 127, 1)
        return (
            (jnp.where(lane == 0, halo_s, r0), jnp.where(lane == 127, q1, q0)),
            (jnp.where(lane == 0, r0, r1), jnp.where(lane == 127, halo_n, q1)),
        )

    def neighbours(g, t, k, v):
        halo_s = roll(centre(g, yh[t, 0]), lax.rem(128 - k, 128), 1)
        halo_n = roll(centre(g, yh[t, 1]), 127 - k, 1)
        ctr = [centre(g, v[c]) for c in range(2)]
        sn = south_north(ctr[0], ctr[1], halo_s, halo_n)
        res = []
        for c in range(2):
            w, e = west_east(
                g, v[c],
                lambda: xh[t, 0, c, pl.ds(k, 1), :],
                lambda: xh[t, 1, c, pl.ds(k, 1), :],
            )
            res.append((ctr[c], w, e) + sn[c])
        return res

    one = jnp.ones((16, 128), F32)
    mask_w = jnp.where(row16 == 0, jnp.where(has_w, 1.0, 0.0).astype(F32), one)
    mask_e = jnp.where(row16 == 15, jnp.where(has_e, 1.0, 0.0).astype(F32), one)
    mask_s = jnp.where(lane == 0, jnp.where(gy > 0, 1.0, 0.0).astype(F32), one)
    mask_n = jnp.where(lane == 127, jnp.where(gy < ny - 1, 1.0, 0.0).astype(F32), one)
    depth2 = 2.0 * ASPECT * ASPECT

    def setup(g):
        top = jnp.where(has_u, depth2, 0.0).astype(F32)
        zero = jnp.zeros((16, 128), F32)
        init = tuple(
            (
                top * recip(centre(g, sg[0, c]) + centre(g, sg[1, c])),
                zero, one, one, zero,
            )
            for c in range(2)
        )

        def body(z, carry):
            near = neighbours(g, 0, 32 + z, [sg[z + 1, c] for c in range(2)])
            res = []
            for c in range(2):
                sh, ratio, gg, rr, s00 = carry[c]
                here, w, e, s, n = near[c]
                lw, le = 2.0 * recip(here + w), 2.0 * recip(here + e)
                ls, ln = 2.0 * recip(here + s), 2.0 * recip(here + n)
                if g == 1:
                    lw, le = lw * mask_w, le * mask_e
                if c == 0:
                    ls = ls * mask_s
                else:
                    ln = ln * mask_n
                dp = depth2 * recip(here + centre(g, sg[z + 2, c]))
                diag = sh + dp + lw + le + ls + ln
                inv = recip(diag - sh * ratio)
                ee = sh * inv
                ratio = dp * inv
                gg = ee * gg
                s00 = s00 + rr * gg
                lw_r[g, z, c], le_r[g, z, c], ls_r[g, z, c], ln_r[g, z, c] = lw, le, ls, ln
                inv_r[g, z, c], rt_r[g, z, c], g_r[g, z, c], r_r[g, z, c] = inv, ratio, gg, rr
                e_r[g, z, c] = jnp.where(z == 0, inv, ee)
                res.append((dp, ratio, gg, rr * ratio, s00))
            return tuple(res)

        last = loop(8, body, init)
        for c in range(2):
            ss[g, 0, c], ss[g, 1, c], ss[g, 2, c], ss[g, 3, c] = (
                last[c][4], last[c][2], last[c][3], last[c][1],
            )

    def forward(g, t, load):
        for half in range(2):
            def body(z, carry):
                res = []
                for i in range(2):
                    s = 2 * half + i
                    near = neighbours(g, t, s * 8 + z, [load(s, z, c) for c in range(2)])
                    for c in range(2):
                        f, first = carry[2 * i + c]
                        here, w, e, so, no = near[c]
                        rhs = (lw_r[g, z, c] * w + le_r[g, z, c] * e) + (
                            ls_r[g, z, c] * so + ln_r[g, z, c] * no
                        )
                        f = rhs * inv_r[g, z, c] + e_r[g, z, c] * f
                        fw[g, s, z, c] = f
                        res.append((f, first + r_r[g, z, c] * f))
                return tuple(res)

            zero = jnp.zeros((16, 128), F32)
            init = tuple(
                (centre(g, src[2 * half + i, c]), zero) for i in range(2) for c in range(2)
            )
            last = loop(8, body, init)
            for i in range(2):
                for c in range(2):
                    ends[g, 1, 2 * half + i, c], ends[g, 0, 2 * half + i, c] = last[2 * i + c]

    i_out, i_in = jnp.where(up, 0, 1), jnp.where(up, 1, 0)
    i_oo, i_oi = jnp.where(up, 0, 3), jnp.where(up, 1, 2)
    i_io, i_ii = jnp.where(up, 2, 1), jnp.where(up, 3, 0)
    end_of = {"gz": jnp.where(up, 0, nz - 1)}
    mid_of = {"gz": jnp.where(up, 1, nz - 2)}
    twin = {"gz": nz - 1 - p}

    def hops(t, g):
        n = 5 if t == 0 else 4
        return (
            remote(m1s.at[t, g, 0:n], m1r.at[t, g, 0:n], ms.at[t, g, 0], mr.at[t, g, 0], mid_of),
            remote(m2s.at[t, g, 0:n], m2r.at[t, g, 0:n], ms.at[t, g, 1], mr.at[t, g, 1], twin),
            remote(m3s.at[t, g], m3r.at[t, g], ms.at[t, g, 2], mr.at[t, g, 2], end_of),
        )

    hop = [[hops(t, g) for g in range(2)] for t in range(2)]
    pairs = [(s, c) for s in range(4) for c in range(2)]

    def end_send(t, g):
        @pl.when(is_end)
        def _():
            for s, c in pairs:
                m1s[t, g, s, c] = ends[g, i_in, s, c]
            if t == 0:
                for c in range(2):
                    m1s[t, g, 4, c] = ss[g, i_ii, c]
            hop[t][g][0].start()

    def mid_forward(t, g):
        @pl.when(is_mid)
        def _():
            hop[t][g][0].wait_recv()
            for c in range(2):
                b_out = m1r[0, g, 4, c]
                if t == 0:
                    q = 1.0 / (1.0 - ss[g, i_oo, c] * b_out)
                    km[g, 0, c] = q
                    km[g, 1, c] = q * ss[g, i_io, c]
                    m2s[0, g, 4, c] = ss[g, i_ii, c] + ss[g, i_oi, c] * b_out * q * ss[g, i_io, c]
                for s in range(4):
                    a_out = m1r[t, g, s, c]
                    first = (ends[g, i_out, s, c] + ss[g, i_oo, c] * a_out) * km[g, 0, c]
                    tt[g, s, c] = first
                    m2s[t, g, s, c] = ends[g, i_in, s, c] + ss[g, i_oi, c] * (a_out + b_out * first)
            hop[t][g][1].start()

    def mid_solve(t, g):
        @pl.when(is_mid)
        def _():
            hop[t][g][1].wait_recv()
            for c in range(2):
                b_out, b_in, b_mine = m1r[0, g, 4, c], m2r[0, g, 4, c], m2s[0, g, 4, c]
                if t == 0:
                    km[g, 2, c] = 1.0 / (1.0 - b_in * b_mine)
                for s in range(4):
                    w_in = (m2r[t, g, s, c] + b_in * m2s[t, g, s, c]) * km[g, 2, c]
                    first = tt[g, s, c] + km[g, 1, c] * w_in
                    m3s[t, g, s, c] = first
                    wab[g, i_in, s, c] = w_in
                    wab[g, i_out, s, c] = m1r[t, g, s, c] + b_out * first
            hop[t][g][2].start()

    def end_solve(t, g):
        @pl.when(is_end)
        def _():
            hop[t][g][2].wait_recv()
            for s, c in pairs:
                wab[g, i_in, s, c] = m3r[t, g, s, c]
                wab[g, i_out, s, c] = jnp.zeros((16, 128), F32)

    def backward(t, g, emit):
        for half in range(2):
            def body(step, carry):
                z = 7 - step
                acc_s, acc_n, w_next = carry
                res = []
                for i in range(2):
                    s = 2 * half + i
                    k = s * 8 + z
                    both = []
                    for c in range(2):
                        w = fw[g, s, z, c] + g_r[g, z, c] * wab[g, 0, s, c] + (
                            rt_r[g, z, c] * w_next[2 * i + c]
                        )
                        res.append(w)
                        v = emit(s, z, c, w)
                        if g == 1:
                            xp[t + 1, 0, c, pl.ds(k, 1), :] = v[0:1]
                            xp[t + 1, 1, c, pl.ds(k, 1), :] = v[15:16]
                        both.append(v)
                    acc_s = jnp.where(lane == k, roll(both[0], k, 1), acc_s)
                    acc_n = jnp.where(lane == k, roll(both[1], k + 1, 1), acc_n)
                return acc_s, acc_n, tuple(res)

            if half == 0:
                zero = jnp.zeros((16, 128), F32)
                acc = (zero, zero)
            first = tuple(wab[g, 1, 2 * half + i, c] for i in range(2) for c in range(2))
            acc = loop(8, body, acc + (first,))[:2]
        for d in range(2):
            if g == 0:
                yp[t + 1, d, 8:24] = acc[d]
            else:
                yp[t + 1, d, 0:8] = acc[d][0:8]
                yp[t + 1, d, 24:32] = acc[d][8:16]

    def put(ref, g, s, z, c, v):
        if g == 0:
            ref[s, z, c, 8:24] = v
        else:
            ref[s, z, c, 0:8] = v[0:8]
            ref[s, z, c, 24:32] = v[8:16]

    def emit_first(g):
        def emit(s, z, c, w):
            put(fp, g, s, z, c, w)
            return w
        return emit

    def emit_relaxed(g):
        rows = (1, 2) if g == 0 else (0, 3)
        def emit(s, z, c, w):
            change = w - centre(g, fp[s, z, c])
            put(ch, g, s, z, c, change)
            for i in range(2):
                on[s, z, c, pl.ds(rows[i], 8, stride=4), :] = w[8 * i:8 * i + 8]
            return change
        return emit

    def load_pot(s, z, c):
        return jnp.concatenate([p_nat[s, z, c, pl.ds(j, 8, stride=4), :] for j in range(4)], 0)

    def load_first(s, z, c):
        return fp[s, z, c]

    def chain(t):
        for g in range(2):
            mid_forward(t, g)
        for g in range(2):
            mid_solve(t, g)
        for g in range(2):
            end_solve(t, g)
            backward(t, g, (emit_first if t == 0 else emit_relaxed)(g))

    wait_y(0)
    pl.when(has_d)(to_above.wait_recv)
    pl.when(has_u)(to_below.wait_recv)
    setup(0)
    forward(0, 0, load_pot)
    end_send(0, 0)
    wait_x(0)
    setup(1)
    forward(1, 0, load_pot)
    end_send(0, 1)
    chain(0)
    send_x(1)
    send_y(1)

    wait_y(1)
    forward(0, 1, load_first)
    end_send(1, 0)
    wait_x(1)
    forward(1, 1, load_first)
    end_send(1, 1)
    chain(1)
    send_x(2)
    send_y(2)
    out_cp = [
        pltpu.make_async_copy(on.at[:, :, c], out.at[:, :, :, c * 128:(c + 1) * 128], loc.at[0, c])
        for c in range(2)
    ]
    for cp in out_cp:
        cp.start()

    lane8 = lax.broadcasted_iota(jnp.int32, (8, 128), 1)
    even = (2 * lane8) % 128

    def squeeze(v):
        return jnp.take_along_axis(v + roll(v, 127, 1), even, axis=1)

    def defect(g):
        def body(z, carry):
            for s in range(4):
                near = neighbours(g, 2, s * 8 + z, [ch[s, z, c] for c in range(2)])
                low, high = [], []
                for c in range(2):
                    here, w, e, so, no = near[c]
                    d = (lw_r[g, z, c] * w + le_r[g, z, c] * e) + (
                        ls_r[g, z, c] * so + ln_r[g, z, c] * no
                    )
                    if g == 0:
                        df[s, z, c] = d
                    else:
                        d = d + df[s, z, c]
                        low.append(squeeze(d[0:8]))
                        high.append(squeeze(d[8:16]))
                if g == 1:
                    co[s, z, pl.ds(0, 8, stride=2), :] = jnp.where(lane8 < 64, low[0], low[1])
                    co[s, z, pl.ds(1, 8, stride=2), :] = jnp.where(lane8 < 64, high[0], high[1])
            return carry

        loop(8, body, 0)

    wait_y(2)
    defect(0)
    wait_x(2)
    defect(1)
    co_cp = pltpu.make_async_copy(co, coarse, loc.at[1, 0])
    co_cp.start()

    pl.when(has_u)(to_above.wait_send)
    pl.when(has_d)(to_below.wait_send)
    for t in range(3):
        pl.when(has_w)(lat[t][0].wait_send)
        pl.when(has_e)(lat[t][1].wait_send)
        lat[t][2].wait_send()
        lat[t][3].wait_send()
    for t in range(2):
        for g in range(2):
            pl.when(is_end)(hop[t][g][0].wait_send)
            pl.when(is_mid)(hop[t][g][1].wait_send)
            pl.when(is_mid)(hop[t][g][2].wait_send)
    for cp in out_cp:
        cp.wait()
    co_cp.wait()


def solution(mesh):
    nz, nx, ny = mesh.shape["gz"], mesh.shape["gx"], mesh.shape["gy"]

    def body(potential, labels, conductivity, electrodes):
        coef = pltpu.VMEM((2, 8, 2, 16, 128), F32)
        field = pltpu.VMEM((4, 8, 2, 32, 128), F32)
        msg5 = pltpu.VMEM((2, 2, 5, 2, 16, 128), F32)
        msg4 = pltpu.VMEM((2, 2, 4, 2, 16, 128), F32)
        dma = pltpu.SemaphoreType.DMA
        return pl.pallas_call(
            functools.partial(kernel, nz, nx, ny),
            out_shape=(
                jax.ShapeDtypeStruct((4, 8, 32, 256), F32),
                jax.ShapeDtypeStruct((4, 8, 16, 128), F32),
            ),
            in_specs=[
                pl.BlockSpec(memory_space=pl.ANY),
                pl.BlockSpec(memory_space=pl.ANY),
                pl.BlockSpec(memory_space=pltpu.SMEM),
                pl.BlockSpec(memory_space=pltpu.SMEM),
            ],
            out_specs=(pl.BlockSpec(memory_space=pl.ANY), pl.BlockSpec(memory_space=pl.ANY)),
            scratch_shapes=[
                field,
                pltpu.VMEM((8, 2, 32, 128), jnp.int32),
                pltpu.VMEM((10, 2, 32, 128), F32),
                pltpu.VMEM((3, 2, 2, 40, 128), F32),
                pltpu.VMEM((3, 2, 2, 40, 128), F32),
                pltpu.VMEM((3, 2, 32, 128), F32),
                pltpu.VMEM((3, 2, 32, 128), F32),
                pltpu.VMEM((4, 2, 32, 128), F32),
                coef, coef, coef, coef, coef, coef, coef, coef, coef,
                pltpu.VMEM((2, 4, 2, 16, 128), F32),
                pltpu.VMEM((2, 4, 8, 2, 16, 128), F32),
                field, field, field,
                pltpu.VMEM((4, 8, 2, 16, 128), F32),
                pltpu.VMEM((4, 8, 16, 128), F32),
                pltpu.VMEM((2, 2, 4, 2, 16, 128), F32),
                pltpu.VMEM((2, 2, 4, 2, 16, 128), F32),
                pltpu.VMEM((2, 3, 2, 16, 128), F32),
                pltpu.VMEM((2, 4, 2, 16, 128), F32),
                msg5, msg5, msg5, msg5, msg4, msg4,
                dma((2, 2)), dma((2,)), dma((2,)),
                dma((3, 2)), dma((3, 2)), dma((3, 2)), dma((3, 2)),
                dma((2, 2, 3)), dma((2, 2, 3)),
            ],
            compiler_params=pltpu.CompilerParams(
                collective_id=0, has_side_effects=True, vmem_limit_bytes=40 * 1024 * 1024,
            ),
        )(potential, labels, conductivity, electrodes)

    return jax.shard_map(
        body,
        mesh=mesh,
        in_specs=(P(None, "gz", "gx", "gy"), P("gz", "gx", "gy"), P(), P()),
        out_specs=(P(None, "gz", "gx", "gy"), P(None, "gz", "gx", "gy")),
        check_vma=False,
    )
```

time: 262 us -> 59.3 us (0.23)
  other arithmetic: 63.6 us -> 0 us
  starting transfers between devices: 59.6 us -> 0 us
  local copies, waits for them, and re-layouts: 63.4 us -> 5.18 us
  Pallas kernels: 0 us -> 53.1 us
  waiting for transfers between devices: 41.4 us -> 0 us
  blocking collectives: 15.7 us -> 0 us
  between operations: 16.1 us -> 0.65 us
    ppermute x18 -> x0, starting transfers between devices: 59.6 us -> none  [the longest x9 34.4 us: with_halo(): lax.ppermute(head, axis, [((i + 1) % count, i) for i in range(ends)])]
    pallas_call x0 -> x1, Pallas kernels: none -> 53.1 us  [body(): pl.pallas_call(functools.partial(kernel, nz, nx, ny), out_shape=(jax.Shap...]
    all_gather x2 -> x0, waiting for transfers between devices: 22.4 us -> none  [relax(): lax.all_gather(value_ends(local_part), 'gz', axis=0, tiled=True)]
    ppermute x18 -> x0, waiting for transfers between devices: 19 us -> none  [the longest x9 19 us: with_halo(): lax.ppermute(tail, axis, [(i, (i + 1) % count) for i in range(ends)])]
    unnamed x267 -> x10, local copies, waits for them, and re-layouts: 23.8 us -> 5.18 us
    add x10 -> x0, other arithmetic: 18.6 us -> none  [the longest x1 10.2 us: lookup(): sigma_cells + jnp.where(labels == label_index, conductivity[label_index],...]
    reduce_sum x1 -> x0, other arithmetic: 17.5 us -> none  [body(): coarse_residual = defect.reshape(source_count, depth_cells, width_x // 2,...]
    all_gather x1 -> x0, blocking collectives: 15.7 us -> none  [relax(): lax.all_gather(spread_ends(spreads), 'gz', axis=0, tiled=True)]
  transfers between devices with their start and end apart: 20 -> 0, of which waited for: 5 -> 0; matrix products, arithmetic and copies ran while one was open for 19% -> 0% of each run, Pallas kernels for 0% -> 0%
where the time goes in v1:
time: 59.3 us; the launch traced here: 59 us
  Pallas kernels  53.1 us (90%)
  local copies, waits for them, and re-layouts  5.18 us (9%)
  between operations  0.65 us (1%)
    pallas_call x1, Pallas kernels, body(): pl.pallas_call(functools.partial(kernel, nz, nx, ny), out_shape=(jax.Shap...  53.1 us
    unnamed x10, local copies, waits for them, and re-layouts  5.18 us

profile of v1, /device:TPU:6, one launch (start us, length us, event | category | flops | bytes accessed | tf_op | source)
XLA Modules:
  0.0 59.0 jit_solution(11860843030403602691)
XLA Ops:
  0.6 0.0 copy-start
  0.6 1.2 %copy-done = f32[4,8,32,256]{3,2,1,0:T(8,128)S(1)} copy-done((f32[4,8,32,256]{3,2,1,0:T(8,128)S(1)}, f32[4,8,32,256]{3,2,1,0:T(8,128)}, u32[]{:S(2)}) %copy-start) | copy-done | bytes 1048600
  1.9 0.0 copy-start.1
  1.9 0.9 %copy-done.1 = s32[8,32,256]{2,1,0:T(8,128)S(1)} copy-done((s32[8,32,256]{2,1,0:T(8,128)S(1)}, s32[8,32,256]{2,1,0:T(8,128)}, u32[]{:S(2)}) %copy-start.1) | copy-done | bytes 262168
  2.8 0.0 copy-start.2
  2.8 0.7 %copy-done.2 = s32[4,4]{1,0:T(4,128)S(1)} copy-done((s32[4,4]{1,0:T(4,128)S(1)}, s32[4,4]{1,0:T(4,128)}, u32[]{:S(2)}) %copy-start.2) | copy-done | bytes 88
  3.5 0.0 copy-start.3
  3.5 0.7 %copy-done.3 = f32[16]{0:T(128)S(1)} copy-done((f32[16]{0:T(128)S(1)}, f32[16]{0:T(128)}, u32[]{:S(2)}) %copy-start.3) | copy-done | bytes 88
  4.1 53.1 %shard_map.59 = (f32[4,8,32,256]{3,2,1,0:T(8,128)S(1)}, f32[4,8,16,128]{3,2,1,0:T(8,128)S(1)}) custom-call(f32[4,8,32,256]{3,2,1,0:T(8,128)S(1)} %copy-done, s32[8,32,256]{2,1,0:T(8,128)S(1)} %copy-done.1, f32[16]{0:T(128)S(1)} %copy-done.3, s32[4,4]{1,0:T(4,128)S(1)} %copy-done.2), custom_call_target="tpu_custom_call" | custom-call | tf_op jit(solution)/shard_map/pallas_call | solution.py:547
  57.3 1.0 %copy.8 = f32[4,8,32,256]{3,2,1,0:T(8,128)} copy(f32[4,8,32,256]{3,2,1,0:T(8,128)S(1)} %get-tuple-element.4) | data formatting | bytes 2097152
  58.3 0.7 %copy.9 = f32[4,8,16,128]{3,2,1,0:T(8,128)} copy(f32[4,8,16,128]{3,2,1,0:T(8,128)S(1)} %get-tuple-element.5) | data formatting | bytes 524288
Async XLA Ops:
  0.6 1.2 %copy-start = (f32[4,8,32,256]{3,2,1,0:T(8,128)S(1)}, f32[4,8,32,256]{3,2,1,0:T(8,128)}, u32[]{:S(2)}) copy-start(f32[4,8,32,256]{3,2,1,0:T(8,128)} %pot.1) | copy-start | bytes 3145732
  1.9 0.9 %copy-start.1 = (s32[8,32,256]{2,1,0:T(8,128)S(1)}, s32[8,32,256]{2,1,0:T(8,128)}, u32[]{:S(2)}) copy-start(s32[8,32,256]{2,1,0:T(8,128)} %lab.1) | copy-start | bytes 786436
  2.8 0.7 %copy-start.2 = (s32[4,4]{1,0:T(4,128)S(1)}, s32[4,4]{1,0:T(4,128)}, u32[]{:S(2)}) copy-start(s32[4,4]{1,0:T(4,128)} %elec.1) | copy-start | bytes 196
  3.5 0.7 %copy-start.3 = (f32[16]{0:T(128)S(1)}, f32[16]{0:T(128)}, u32[]{:S(2)}) copy-start(f32[16]{0:T(128)} %cond.1) | copy-start | bytes 196

commit v2 on v1

--- a/solution.py
+++ b/solution.py
@@ -10,7 +10,7 @@
 ASPECT = 128
 MESH = pl.DeviceIdType.MESH
 F32 = jnp.float32
-UNROLL = False
+UNROLL = True
 
 
 def roll(v, shift, axis):
@@ -109,12 +109,6 @@
     def _():
         sg[9] = sg[8]
 
-    pl.semaphore_wait(
-        barrier,
-        2 + has_w.astype(jnp.int32) + has_e.astype(jnp.int32)
-        + has_u.astype(jnp.int32) + has_d.astype(jnp.int32),
-    )
-
     def remote(src_ref, dst_ref, send, recv, device):
         return pltpu.make_async_remote_copy(
             src_ref=src_ref, dst_ref=dst_ref, send_sem=send, recv_sem=recv,
@@ -123,8 +117,6 @@
 
     to_above = remote(sg.at[1], sg.at[9], zs.at[0], zr.at[1], above)
     to_below = remote(sg.at[8], sg.at[0], zs.at[1], zr.at[0], below)
-    pl.when(has_u)(to_above.start)
-    pl.when(has_d)(to_below.start)
 
     def lateral_copies(t):
         n = 40 if t == 0 else 32
@@ -184,8 +176,16 @@
         return acc_s, acc_n
 
     acc = loop(8, pack_pot, acc)
+    yp[0, 0], yp[0, 1] = acc
+    pl.semaphore_wait(
+        barrier,
+        2 + has_w.astype(jnp.int32) + has_e.astype(jnp.int32)
+        + has_u.astype(jnp.int32) + has_d.astype(jnp.int32),
+    )
+
     send_x(0)
-    yp[0, 0], yp[0, 1] = acc
+    pl.when(has_u)(to_above.start)
+    pl.when(has_d)(to_below.start)
     send_y(0)
 
     here = jnp.where(p == 0, 4.0 * ASPECT, 0.0).astype(F32)
@@ -582,7 +582,7 @@
                 dma((2, 2, 3)), dma((2, 2, 3)),
             ],
             compiler_params=pltpu.CompilerParams(
-                collective_id=0, has_side_effects=True, vmem_limit_bytes=40 * 1024 * 1024,
+                collective_id=0, has_side_effects=True, vmem_limit_bytes=60 * 1024 * 1024,
             ),
         )(potential, labels, conductivity, electrodes)
 

time: 59.3 us -> 53.2 us (0.90)
  Pallas kernels: 53.1 us -> 49.4 us
  local copies, waits for them, and re-layouts: 5.18 us -> 3.06 us
    pallas_call x1, Pallas kernels: 53.1 us -> 49.4 us  [body(): pl.pallas_call(functools.partial(kernel, nz, nx, ny), out_shape=(jax.Shap...]
    unnamed x10 -> x4, local copies, waits for them, and re-layouts: 5.18 us -> 3.06 us
where the time goes in v2:
time: 53.2 us; the launch traced here: 53.1 us
  Pallas kernels  49.4 us (93%)
  local copies, waits for them, and re-layouts  3.06 us (6%)
  between operations  0.65 us (1%)
    pallas_call x1, Pallas kernels, body(): pl.pallas_call(functools.partial(kernel, nz, nx, ny), out_shape=(jax.Shap...  49.4 us
    unnamed x4, local copies, waits for them, and re-layouts  3.06 us

profile of v2, /device:TPU:6, one launch (start us, length us, event | category | flops | bytes accessed | tf_op | source)
XLA Modules:
  0.0 53.1 jit_solution(16519411884796035590)
XLA Ops:
  0.6 49.4 %shard_map.59 = (f32[4,8,32,256]{3,2,1,0:T(8,128)}, f32[4,8,16,128]{3,2,1,0:T(8,128)}) custom-call(f32[4,8,32,256]{3,2,1,0:T(8,128)} %pot.1, s32[8,32,256]{2,1,0:T(8,128)} %lab.1, f32[16]{0:T(128)} %cond.1, s32[4,4]{1,0:T(4,128)} %elec.1), custom_call_target="tpu_custom_call" | custom-call | tf_op jit(solution)/shard_map/pallas_call | solution.py:547
  50.0 0.0 copy-start
  50.0 2.4 %copy.8 = f32[4,8,32,256]{3,2,1,0:T(8,128)} copy(f32[4,8,32,256]{3,2,1,0:T(8,128)} %get-tuple-element.4) | data formatting | bytes 2097152
  52.4 0.0 copy-done
  52.4 0.7 %copy.9 = f32[4,8,16,128]{3,2,1,0:T(8,128)} copy(f32[4,8,16,128]{3,2,1,0:T(8,128)S(1)} %copy-done) | data formatting | bytes 524288
Async XLA Ops:
  50.0 2.4 %copy-start = (f32[4,8,16,128]{3,2,1,0:T(8,128)S(1)}, f32[4,8,16,128]{3,2,1,0:T(8,128)}, u32[]{:S(2)}) copy-start(f32[4,8,16,128]{3,2,1,0:T(8,128)} %get-tuple-element.5) | copy-start | bytes 786436

commit v3 on v2

--- a/solution.py
+++ b/solution.py
@@ -35,8 +35,8 @@
     p_nat, l_nat, sg, xp, xh, yp, yh, src,
     lw_r, le_r, ls_r, ln_r, inv_r, e_r, rt_r, g_r, r_r, ss,
     fw, fp, ch, on, df, co, ends, wab, km, tt,
-    m1s, m1r, m2s, m2r, m3s, m3r,
-    loc, zs, zr, xs, xr, ys, yr, ms, mr,
+    m0s, m0r, m1s, m1r, m2s, m2r, b2s, b2r, m3s, m3r, b3s, b3r, ods, ids, xin, kx,
+    loc, zs, zr, xs, xr, ys, yr, ms, mr, bs, br, qs, qr,
 ):
     p = lax.axis_index("gz")
     gx = lax.axis_index("gx")
@@ -80,7 +80,9 @@
 
     greet(south)
     greet(north)
-    for cond_here, device in ((has_w, west), (has_e, east), (has_u, above), (has_d, below)):
+    for step in range(1, nz):
+        greet({"gz": lax.rem(p + step, nz)})
+    for cond_here, device in ((has_w, west), (has_e, east)):
         pl.when(cond_here)(functools.partial(greet, device))
 
     for cp in lab_cp:
@@ -115,6 +117,15 @@
             device_id=device, device_id_type=MESH,
         )
 
+    started = []
+
+    def start(copy, where=None):
+        started.append((copy, where))
+        if where is None:
+            copy.start()
+        else:
+            pl.when(where)(copy.start)
+
     to_above = remote(sg.at[1], sg.at[9], zs.at[0], zr.at[1], above)
     to_below = remote(sg.at[8], sg.at[0], zs.at[1], zr.at[0], below)
 
@@ -130,12 +141,12 @@
     lat = [lateral_copies(t) for t in range(3)]
 
     def send_x(t):
-        pl.when(has_w)(lat[t][0].start)
-        pl.when(has_e)(lat[t][1].start)
+        start(lat[t][0], has_w)
+        start(lat[t][1], has_e)
 
     def send_y(t):
-        lat[t][2].start()
-        lat[t][3].start()
+        start(lat[t][2])
+        start(lat[t][3])
 
     def wait_x(t):
         pl.when(has_e)(lat[t][0].wait_recv)
@@ -179,13 +190,12 @@
     yp[0, 0], yp[0, 1] = acc
     pl.semaphore_wait(
         barrier,
-        2 + has_w.astype(jnp.int32) + has_e.astype(jnp.int32)
-        + has_u.astype(jnp.int32) + has_d.astype(jnp.int32),
+        nz + 1 + has_w.astype(jnp.int32) + has_e.astype(jnp.int32),
     )
 
     send_x(0)
-    pl.when(has_u)(to_above.start)
-    pl.when(has_d)(to_below.start)
+    start(to_above, has_u)
+    start(to_below, has_d)
     send_y(0)
 
     here = jnp.where(p == 0, 4.0 * ASPECT, 0.0).astype(F32)
@@ -281,8 +291,8 @@
                 last[c][4], last[c][2], last[c][3], last[c][1],
             )
 
-    def forward(g, t, load):
-        for half in range(2):
+    def forward(g, t, half, load):
+        if True:
             def body(z, carry):
                 res = []
                 for i in range(2):
@@ -314,99 +324,191 @@
     end_of = {"gz": jnp.where(up, 0, nz - 1)}
     mid_of = {"gz": jnp.where(up, 1, nz - 2)}
     twin = {"gz": nz - 1 - p}
-
-    def hops(t, g):
-        n = 5 if t == 0 else 4
+    mate = {"gz": jnp.where(lax.rem(p, 2) == 0, p + 1, p - 1)}
+    far_mid = {"gz": jnp.where(up, nz - 2, 1)}
+    far_end = {"gz": jnp.where(up, nz - 1, 0)}
+    i_od = jnp.where(is_end, i_in, i_out)
+    slot = jnp.where(is_end, 2, 1)
+
+    def hops(g, h):
         return (
-            remote(m1s.at[t, g, 0:n], m1r.at[t, g, 0:n], ms.at[t, g, 0], mr.at[t, g, 0], mid_of),
-            remote(m2s.at[t, g, 0:n], m2r.at[t, g, 0:n], ms.at[t, g, 1], mr.at[t, g, 1], twin),
-            remote(m3s.at[t, g], m3r.at[t, g], ms.at[t, g, 2], mr.at[t, g, 2], end_of),
+            remote(m1s.at[g, h], m1r.at[g, h], ms.at[g, h, 0], mr.at[g, h, 0], mid_of),
+            remote(m2s.at[g, h], m2r.at[g, h], ms.at[g, h, 1], mr.at[g, h, 1], twin),
+            remote(m3s.at[g, h], m3r.at[g, h], ms.at[g, h, 2], mr.at[g, h, 2], end_of),
         )
 
-    hop = [[hops(t, g) for g in range(2)] for t in range(2)]
-    pairs = [(s, c) for s in range(4) for c in range(2)]
-
-    def end_send(t, g):
+    def factor_hops(g):
+        return (
+            remote(m0s.at[g], m0r.at[g], bs.at[g, 0], br.at[g, 0], mid_of),
+            remote(b2s.at[g], b2r.at[g], bs.at[g, 1], br.at[g, 1], twin),
+            remote(b3s.at[g], b3r.at[g], bs.at[g, 2], br.at[g, 2], end_of),
+        )
+
+    def cross(g, h):
+        def one_of(src_ref, at, i, device):
+            return remote(src_ref.at[g, h], xin.at[g, h, at], qs.at[g, h, i], qr.at[g, h, at], device)
+        return (
+            one_of(ids, slot, 0, far_mid), one_of(ids, slot, 1, far_end), one_of(ods, 0, 2, mate),
+        )
+
+    hop = [[hops(g, h) for h in range(2)] for g in range(2)]
+    fhop = [factor_hops(g) for g in range(2)]
+    pairs = [(i, c) for i in range(2) for c in range(2)]
+
+    def end_factor(g):
         @pl.when(is_end)
         def _():
-            for s, c in pairs:
-                m1s[t, g, s, c] = ends[g, i_in, s, c]
-            if t == 0:
+            m0s[g] = ss[g, i_ii]
+        start(fhop[g][0], is_end)
+
+    def end_send(g, h):
+        @pl.when(is_end)
+        def _():
+            for i, c in pairs:
+                m1s[g, h, i, c] = ends[g, i_in, 2 * h + i, c]
+        start(hop[g][h][0], is_end)
+
+    def mid_factor(g):
+        @pl.when(is_mid)
+        def _():
+            fhop[g][0].wait_recv()
+            for c in range(2):
+                b_out = m0r[g, c]
+                q = 1.0 / (1.0 - ss[g, i_oo, c] * b_out)
+                km[g, 0, c] = q
+                km[g, 1, c] = q * ss[g, i_io, c]
+                b2s[g, 0, c] = ss[g, i_ii, c] + ss[g, i_oi, c] * b_out * q * ss[g, i_io, c]
+                b2s[g, 1, c] = ss[g, i_oi, c] * q
+        start(fhop[g][1], is_mid)
+
+    def mid_forward(g, h):
+        @pl.when(is_mid)
+        def _():
+            hop[g][h][0].wait_recv()
+            for i, c in pairs:
+                s = 2 * h + i
+                a_out = m1r[g, h, i, c]
+                first = (ends[g, i_out, s, c] + ss[g, i_oo, c] * a_out) * km[g, 0, c]
+                tt[g, s, c] = first
+                m2s[g, h, i, c] = ends[g, i_in, s, c] + ss[g, i_oi, c] * (a_out + m0r[g, c] * first)
+        start(hop[g][h][1], is_mid)
+
+    def mid_match(g):
+        @pl.when(is_mid)
+        def _():
+            fhop[g][1].wait_recv()
+            for c in range(2):
+                km[g, 2, c] = 1.0 / (1.0 - b2r[g, 0, c] * b2s[g, 0, c])
+
+    def mid_solve(g, h):
+        @pl.when(is_mid)
+        def _():
+            hop[g][h][1].wait_recv()
+            for i, c in pairs:
+                s = 2 * h + i
+                w_in = (m2r[g, h, i, c] + b2r[g, 0, c] * m2s[g, h, i, c]) * km[g, 2, c]
+                first = tt[g, s, c] + km[g, 1, c] * w_in
+                m3s[g, h, i, c] = first
+                wab[g, i_in, s, c] = w_in
+                wab[g, i_out, s, c] = m1r[g, h, i, c] + m0r[g, c] * first
+        start(hop[g][h][2], is_mid)
+
+    def end_solve(g, h):
+        @pl.when(is_end)
+        def _():
+            hop[g][h][2].wait_recv()
+            for i, c in pairs:
+                wab[g, i_in, 2 * h + i, c] = m3r[g, h, i, c]
+                wab[g, i_out, 2 * h + i, c] = jnp.zeros((16, 128), F32)
+
+    def mid_extra(g):
+        @pl.when(is_mid)
+        def _():
+            for c in range(2):
+                b_out, b_in, q = m0r[g, c], b2r[g, 0, c], km[g, 0, c]
+                s_oo, s_oi, s_io, s_ii = ss[g, i_oo, c], ss[g, i_oi, c], ss[g, i_io, c], ss[g, i_ii, c]
+                g_mine, g_in, match = b2s[g, 1, c], b2r[g, 1, c], km[g, 2, c]
+                r = 1.0 / (1.0 - s_ii * b_in)
+                h = s_io * r
+                b3s[g, 0, c] = s_oo + h * b_in * s_oi
+                b3s[g, 1, c] = h
+                b3s[g, 2, c] = h * g_in
+                kx[g, 0, c] = match * b_in
+                kx[g, 1, c] = match * b_in * g_mine
+                kx[g, 2, c] = match
+                kx[g, 3, c] = match * g_in
+                kx[g, 4, c] = q
+                kx[g, 5, c] = b_out * q
+                kx[g, 6, c] = b_out * q * s_io
+                kx[g, 7, c] = s_oi * b_out * q
+                kx[g, 8, c] = h * b_in
+        start(fhop[g][2], is_mid)
+
+    def end_extra(g):
+        @pl.when(is_end)
+        def _():
+            fhop[g][2].wait_recv()
+            for c in range(2):
+                c_in = b3r[g, 0, c]
+                k = 1.0 / (1.0 - c_in * ss[g, i_ii, c])
+                kx[g, 0, c] = k * c_in
+                kx[g, 1, c] = k
+                kx[g, 2, c] = k * b3r[g, 1, c]
+                kx[g, 3, c] = k * b3r[g, 2, c]
+                for i in range(4, 9):
+                    kx[g, i, c] = jnp.zeros((16, 128), F32)
+
+    def cross_send(g, h):
+        for i, c in pairs:
+            s = 2 * h + i
+            ids[g, h, i, c] = ends[g, i_in, s, c] + kx[g, 7, c] * ends[g, i_out, s, c]
+            ods[g, h, i, c] = ends[g, i_od, s, c] + kx[g, 8, c] * ends[g, i_in, s, c]
+        for copy in cross(g, h):
+            start(copy)
+
+    def cross_solve(g, h):
+        for at in range(3):
+            remote(
+                ids.at[g, h], xin.at[g, h, at], qs.at[g, h, 0], qr.at[g, h, at], far_mid
+            ).wait_recv()
+        for i, c in pairs:
+            s = 2 * h + i
+            near, r1, r2 = xin[g, h, 0, i, c], xin[g, h, 1, i, c], xin[g, h, 2, i, c]
+            w_in = (kx[g, 0, c] * ids[g, h, i, c] + kx[g, 1, c] * near) + (
+                kx[g, 2, c] * r1 + kx[g, 3, c] * r2
+            )
+            wab[g, i_in, s, c] = w_in
+            wab[g, i_out, s, c] = (
+                kx[g, 4, c] * near + kx[g, 5, c] * ends[g, i_out, s, c] + kx[g, 6, c] * w_in
+            )
+
+    def backward(t, g, h, emit, acc):
+        def body(step, carry):
+            z = 7 - step
+            acc_s, acc_n, w_next = carry
+            res = []
+            for i in range(2):
+                s = 2 * h + i
+                k = s * 8 + z
+                both = []
                 for c in range(2):
-                    m1s[t, g, 4, c] = ss[g, i_ii, c]
-            hop[t][g][0].start()
-
-    def mid_forward(t, g):
-        @pl.when(is_mid)
-        def _():
-            hop[t][g][0].wait_recv()
-            for c in range(2):
-                b_out = m1r[0, g, 4, c]
-                if t == 0:
-                    q = 1.0 / (1.0 - ss[g, i_oo, c] * b_out)
-                    km[g, 0, c] = q
-                    km[g, 1, c] = q * ss[g, i_io, c]
-                    m2s[0, g, 4, c] = ss[g, i_ii, c] + ss[g, i_oi, c] * b_out * q * ss[g, i_io, c]
-                for s in range(4):
-                    a_out = m1r[t, g, s, c]
-                    first = (ends[g, i_out, s, c] + ss[g, i_oo, c] * a_out) * km[g, 0, c]
-                    tt[g, s, c] = first
-                    m2s[t, g, s, c] = ends[g, i_in, s, c] + ss[g, i_oi, c] * (a_out + b_out * first)
-            hop[t][g][1].start()
-
-    def mid_solve(t, g):
-        @pl.when(is_mid)
-        def _():
-            hop[t][g][1].wait_recv()
-            for c in range(2):
-                b_out, b_in, b_mine = m1r[0, g, 4, c], m2r[0, g, 4, c], m2s[0, g, 4, c]
-                if t == 0:
-                    km[g, 2, c] = 1.0 / (1.0 - b_in * b_mine)
-                for s in range(4):
-                    w_in = (m2r[t, g, s, c] + b_in * m2s[t, g, s, c]) * km[g, 2, c]
-                    first = tt[g, s, c] + km[g, 1, c] * w_in
-                    m3s[t, g, s, c] = first
-                    wab[g, i_in, s, c] = w_in
-                    wab[g, i_out, s, c] = m1r[t, g, s, c] + b_out * first
-            hop[t][g][2].start()
-
-    def end_solve(t, g):
-        @pl.when(is_end)
-        def _():
-            hop[t][g][2].wait_recv()
-            for s, c in pairs:
-                wab[g, i_in, s, c] = m3r[t, g, s, c]
-                wab[g, i_out, s, c] = jnp.zeros((16, 128), F32)
-
-    def backward(t, g, emit):
-        for half in range(2):
-            def body(step, carry):
-                z = 7 - step
-                acc_s, acc_n, w_next = carry
-                res = []
-                for i in range(2):
-                    s = 2 * half + i
-                    k = s * 8 + z
-                    both = []
-                    for c in range(2):
-                        w = fw[g, s, z, c] + g_r[g, z, c] * wab[g, 0, s, c] + (
-                            rt_r[g, z, c] * w_next[2 * i + c]
-                        )
-                        res.append(w)
-                        v = emit(s, z, c, w)
-                        if g == 1:
-                            xp[t + 1, 0, c, pl.ds(k, 1), :] = v[0:1]
-                            xp[t + 1, 1, c, pl.ds(k, 1), :] = v[15:16]
-                        both.append(v)
-                    acc_s = jnp.where(lane == k, roll(both[0], k, 1), acc_s)
-                    acc_n = jnp.where(lane == k, roll(both[1], k + 1, 1), acc_n)
-                return acc_s, acc_n, tuple(res)
-
-            if half == 0:
-                zero = jnp.zeros((16, 128), F32)
-                acc = (zero, zero)
-            first = tuple(wab[g, 1, 2 * half + i, c] for i in range(2) for c in range(2))
-            acc = loop(8, body, acc + (first,))[:2]
+                    w = fw[g, s, z, c] + g_r[g, z, c] * wab[g, 0, s, c] + (
+                        rt_r[g, z, c] * w_next[2 * i + c]
+                    )
+                    res.append(w)
+                    v = emit(s, z, c, w)
+                    if g == 1:
+                        xp[t + 1, 0, c, pl.ds(k, 1), :] = v[0:1]
+                        xp[t + 1, 1, c, pl.ds(k, 1), :] = v[15:16]
+                    both.append(v)
+                acc_s = jnp.where(lane == k, roll(both[0], k, 1), acc_s)
+                acc_n = jnp.where(lane == k, roll(both[1], k + 1, 1), acc_n)
+            return acc_s, acc_n, tuple(res)
+
+        first = tuple(wab[g, 1, 2 * h + i, c] for i in range(2) for c in range(2))
+        return loop(8, body, acc + (first,))[:2]
+
+    def pack_y(t, g, acc):
         for d in range(2):
             if g == 0:
                 yp[t + 1, d, 8:24] = acc[d]
@@ -443,36 +545,56 @@
     def load_first(s, z, c):
         return fp[s, z, c]
 
-    def chain(t):
-        for g in range(2):
-            mid_forward(t, g)
-        for g in range(2):
-            mid_solve(t, g)
-        for g in range(2):
-            end_solve(t, g)
-            backward(t, g, (emit_first if t == 0 else emit_relaxed)(g))
+    empty = (jnp.zeros((16, 128), F32),) * 2
 
     wait_y(0)
     pl.when(has_d)(to_above.wait_recv)
     pl.when(has_u)(to_below.wait_recv)
     setup(0)
-    forward(0, 0, load_pot)
-    end_send(0, 0)
+    end_factor(0)
+    for h in range(2):
+        forward(0, 0, h, load_pot)
+        end_send(0, h)
     wait_x(0)
     setup(1)
-    forward(1, 0, load_pot)
-    end_send(0, 1)
-    chain(0)
+    end_factor(1)
+    for h in range(2):
+        forward(1, 0, h, load_pot)
+        end_send(1, h)
+    for g in range(2):
+        mid_factor(g)
+        for h in range(2):
+            mid_forward(g, h)
+    for g in range(2):
+        mid_match(g)
+        acc = empty
+        for h in range(2):
+            mid_solve(g, h)
+        for h in range(2):
+            end_solve(g, h)
+            acc = backward(0, g, h, emit_first(g), acc)
+        pack_y(0, g, acc)
     send_x(1)
     send_y(1)
+    for g in range(2):
+        mid_extra(g)
+    for g in range(2):
+        end_extra(g)
 
     wait_y(1)
-    forward(0, 1, load_first)
-    end_send(1, 0)
+    for h in range(2):
+        forward(0, 1, h, load_first)
+        cross_send(0, h)
     wait_x(1)
-    forward(1, 1, load_first)
-    end_send(1, 1)
-    chain(1)
+    for h in range(2):
+        forward(1, 1, h, load_first)
+        cross_send(1, h)
+    for g in range(2):
+        acc = empty
+        for h in range(2):
+            cross_solve(g, h)
+            acc = backward(1, g, h, emit_relaxed(g), acc)
+        pack_y(1, g, acc)
     send_x(2)
     send_y(2)
     out_cp = [
@@ -518,18 +640,11 @@
     co_cp = pltpu.make_async_copy(co, coarse, loc.at[1, 0])
     co_cp.start()
 
-    pl.when(has_u)(to_above.wait_send)
-    pl.when(has_d)(to_below.wait_send)
-    for t in range(3):
-        pl.when(has_w)(lat[t][0].wait_send)
-        pl.when(has_e)(lat[t][1].wait_send)
-        lat[t][2].wait_send()
-        lat[t][3].wait_send()
-    for t in range(2):
-        for g in range(2):
-            pl.when(is_end)(hop[t][g][0].wait_send)
-            pl.when(is_mid)(hop[t][g][1].wait_send)
-            pl.when(is_mid)(hop[t][g][2].wait_send)
+    for copy, where in started:
+        if where is None:
+            copy.wait_send()
+        else:
+            pl.when(where)(copy.wait_send)
     for cp in out_cp:
         cp.wait()
     co_cp.wait()
@@ -541,8 +656,10 @@
     def body(potential, labels, conductivity, electrodes):
         coef = pltpu.VMEM((2, 8, 2, 16, 128), F32)
         field = pltpu.VMEM((4, 8, 2, 32, 128), F32)
-        msg5 = pltpu.VMEM((2, 2, 5, 2, 16, 128), F32)
-        msg4 = pltpu.VMEM((2, 2, 4, 2, 16, 128), F32)
+        msg = pltpu.VMEM((2, 2, 2, 2, 16, 128), F32)
+        part1 = pltpu.VMEM((2, 2, 16, 128), F32)
+        part2 = pltpu.VMEM((2, 2, 2, 16, 128), F32)
+        part3 = pltpu.VMEM((2, 3, 2, 16, 128), F32)
         dma = pltpu.SemaphoreType.DMA
         return pl.pallas_call(
             functools.partial(kernel, nz, nx, ny),
@@ -576,9 +693,12 @@
                 pltpu.VMEM((2, 2, 4, 2, 16, 128), F32),
                 pltpu.VMEM((2, 3, 2, 16, 128), F32),
                 pltpu.VMEM((2, 4, 2, 16, 128), F32),
-                msg5, msg5, msg5, msg5, msg4, msg4,
+                part1, part1, msg, msg, msg, msg, part2, part2, msg, msg, part3, part3, msg, msg,
+                pltpu.VMEM((2, 2, 3, 2, 2, 16, 128), F32),
+                pltpu.VMEM((2, 9, 2, 16, 128), F32),
                 dma((2, 2)), dma((2,)), dma((2,)),
                 dma((3, 2)), dma((3, 2)), dma((3, 2)), dma((3, 2)),
+                dma((2, 2, 3)), dma((2, 2, 3)), dma((2, 3)), dma((2, 3)),
                 dma((2, 2, 3)), dma((2, 2, 3)),
             ],
             compiler_params=pltpu.CompilerParams(

time: 53.2 us -> 48 us (0.902)
  Pallas kernels: 49.4 us -> 43.8 us
    pallas_call x1, Pallas kernels: 49.4 us -> 43.8 us  [body(): pl.pallas_call(functools.partial(kernel, nz, nx, ny), out_shape=(jax.Shap...]
where the time goes in v3:
time: 48 us; the launch traced here: 47.5 us
  Pallas kernels  43.8 us (91%)
  local copies, waits for them, and re-layouts  3.06 us (6%)
  between operations  0.65 us (1%)
    pallas_call x1, Pallas kernels, body(): pl.pallas_call(functools.partial(kernel, nz, nx, ny), out_shape=(jax.Shap...  43.8 us
    unnamed x4, local copies, waits for them, and re-layouts  3.06 us

profile of v3, /device:TPU:6, one launch (start us, length us, event | category | flops | bytes accessed | tf_op | source)
XLA Modules:
  0.0 47.5 jit_solution(5807118369522253359)
XLA Ops:
  0.6 43.8 %shard_map.59 = (f32[4,8,32,256]{3,2,1,0:T(8,128)}, f32[4,8,16,128]{3,2,1,0:T(8,128)}) custom-call(f32[4,8,32,256]{3,2,1,0:T(8,128)} %pot.1, s32[8,32,256]{2,1,0:T(8,128)} %lab.1, f32[16]{0:T(128)} %cond.1, s32[4,4]{1,0:T(4,128)} %elec.1), custom_call_target="tpu_custom_call" | custom-call | tf_op jit(solution)/shard_map/pallas_call | solution.py:664
  44.5 0.0 copy-start
  44.5 2.4 %copy.8 = f32[4,8,32,256]{3,2,1,0:T(8,128)} copy(f32[4,8,32,256]{3,2,1,0:T(8,128)} %get-tuple-element.4) | data formatting | bytes 2097152
  46.8 0.0 copy-done
  46.8 0.7 %copy.9 = f32[4,8,16,128]{3,2,1,0:T(8,128)} copy(f32[4,8,16,128]{3,2,1,0:T(8,128)S(1)} %copy-done) | data formatting | bytes 524288
Async XLA Ops:
  44.5 2.4 %copy-start = (f32[4,8,16,128]{3,2,1,0:T(8,128)S(1)}, f32[4,8,16,128]{3,2,1,0:T(8,128)}, u32[]{:S(2)}) copy-start(f32[4,8,16,128]{3,2,1,0:T(8,128)} %get-tuple-element.5) | copy-start | bytes 786436

commit v4 on v3

--- a/solution.py
+++ b/solution.py
@@ -604,17 +604,17 @@
     for cp in out_cp:
         cp.start()
 
-    lane8 = lax.broadcasted_iota(jnp.int32, (8, 128), 1)
-    even = (2 * lane8) % 128
-
-    def squeeze(v):
-        return jnp.take_along_axis(v + roll(v, 127, 1), even, axis=1)
+    pick = (
+        lax.broadcasted_iota(jnp.int32, (256, 128), 0) // 2
+        == lax.broadcasted_iota(jnp.int32, (256, 128), 1)
+    ).astype(F32)
 
     def defect(g):
         def body(z, carry):
+            rows = []
             for s in range(4):
                 near = neighbours(g, 2, s * 8 + z, [ch[s, z, c] for c in range(2)])
-                low, high = [], []
+                both = []
                 for c in range(2):
                     here, w, e, so, no = near[c]
                     d = (lw_r[g, z, c] * w + le_r[g, z, c] * e) + (
@@ -623,12 +623,17 @@
                     if g == 0:
                         df[s, z, c] = d
                     else:
-                        d = d + df[s, z, c]
-                        low.append(squeeze(d[0:8]))
-                        high.append(squeeze(d[8:16]))
+                        both.append(d + df[s, z, c])
                 if g == 1:
-                    co[s, z, pl.ds(0, 8, stride=2), :] = jnp.where(lane8 < 64, low[0], low[1])
-                    co[s, z, pl.ds(1, 8, stride=2), :] = jnp.where(lane8 < 64, high[0], high[1])
+                    rows.append(jnp.concatenate(both, 1))
+            if g == 1:
+                d = jnp.dot(
+                    jnp.concatenate(rows, 0), pick,
+                    precision=lax.Precision.HIGHEST, preferred_element_type=F32,
+                )
+                for s in range(4):
+                    co[s, z, pl.ds(0, 8, stride=2), :] = d[16 * s:16 * s + 8]
+                    co[s, z, pl.ds(1, 8, stride=2), :] = d[16 * s + 8:16 * s + 16]
             return carry
 
         loop(8, body, 0)

time: 48 us -> 44.8 us (0.933)
  Pallas kernels: 43.8 us -> 40.6 us
    pallas_call x1, Pallas kernels: 43.8 us -> 40.6 us  [body(): pl.pallas_call(functools.partial(kernel, nz, nx, ny), out_shape=(jax.Shap...]
where the time goes in v4:
time: 44.8 us; the launch traced here: 44.3 us
  Pallas kernels  40.6 us (91%)
  local copies, waits for them, and re-layouts  3.06 us (7%)
  between operations  0.65 us (1%)
    pallas_call x1, Pallas kernels, body(): pl.pallas_call(functools.partial(kernel, nz, nx, ny), out_shape=(jax.Shap...  40.6 us
    unnamed x4, local copies, waits for them, and re-layouts  3.06 us

profile of v4, /device:TPU:6, one launch (start us, length us, event | category | flops | bytes accessed | tf_op | source)
XLA Modules:
  0.0 44.3 jit_solution(12358052863101535220)
XLA Ops:
  0.6 40.6 %shard_map.59 = (f32[4,8,32,256]{3,2,1,0:T(8,128)}, f32[4,8,16,128]{3,2,1,0:T(8,128)}) custom-call(f32[4,8,32,256]{3,2,1,0:T(8,128)} %pot.1, s32[8,32,256]{2,1,0:T(8,128)} %lab.1, f32[16]{0:T(128)} %cond.1, s32[4,4]{1,0:T(4,128)} %elec.1), custom_call_target="tpu_custom_call" | custom-call | tf_op jit(solution)/shard_map/pallas_call | solution.py:669
  41.2 0.0 copy-start
  41.3 2.4 %copy.8 = f32[4,8,32,256]{3,2,1,0:T(8,128)} copy(f32[4,8,32,256]{3,2,1,0:T(8,128)} %get-tuple-element.4) | data formatting | bytes 2097152
  43.6 0.0 copy-done
  43.6 0.7 %copy.9 = f32[4,8,16,128]{3,2,1,0:T(8,128)} copy(f32[4,8,16,128]{3,2,1,0:T(8,128)S(1)} %copy-done) | data formatting | bytes 524288
Async XLA Ops:
  41.2 2.4 %copy-start = (f32[4,8,16,128]{3,2,1,0:T(8,128)S(1)}, f32[4,8,16,128]{3,2,1,0:T(8,128)}, u32[]{:S(2)}) copy-start(f32[4,8,16,128]{3,2,1,0:T(8,128)} %get-tuple-element.5) | copy-start | bytes 786436

commit v5 on v4

--- a/solution.py
+++ b/solution.py
@@ -655,6 +655,22 @@
     co_cp.wait()
 
 
+def store_kernel(relaxed, restricted, out, coarse, held, held_coarse, sems):
+    fetch = [pltpu.make_async_copy(restricted, held_coarse, sems.at[0, 4])] + [
+        pltpu.make_async_copy(relaxed.at[s], held.at[s], sems.at[0, s]) for s in range(4)
+    ]
+    store = [pltpu.make_async_copy(held_coarse, coarse, sems.at[1, 4])] + [
+        pltpu.make_async_copy(held.at[s], out.at[s], sems.at[1, s]) for s in range(4)
+    ]
+    for cp in fetch:
+        cp.start()
+    for cp, then in zip(fetch, store):
+        cp.wait()
+        then.start()
+    for cp in store:
+        cp.wait()
+
+
 def solution(mesh):
     nz, nx, ny = mesh.shape["gz"], mesh.shape["gx"], mesh.shape["gy"]
 
@@ -666,12 +682,14 @@
         part2 = pltpu.VMEM((2, 2, 2, 16, 128), F32)
         part3 = pltpu.VMEM((2, 3, 2, 16, 128), F32)
         dma = pltpu.SemaphoreType.DMA
-        return pl.pallas_call(
+        shapes = (
+            jax.ShapeDtypeStruct((4, 8, 32, 256), F32),
+            jax.ShapeDtypeStruct((4, 8, 16, 128), F32),
+        )
+        anywhere = pl.BlockSpec(memory_space=pl.ANY)
+        results = pl.pallas_call(
             functools.partial(kernel, nz, nx, ny),
-            out_shape=(
-                jax.ShapeDtypeStruct((4, 8, 32, 256), F32),
-                jax.ShapeDtypeStruct((4, 8, 16, 128), F32),
-            ),
+            out_shape=shapes,
             in_specs=[
                 pl.BlockSpec(memory_space=pl.ANY),
                 pl.BlockSpec(memory_space=pl.ANY),
@@ -710,6 +728,17 @@
                 collective_id=0, has_side_effects=True, vmem_limit_bytes=60 * 1024 * 1024,
             ),
         )(potential, labels, conductivity, electrodes)
+        return pl.pallas_call(
+            store_kernel,
+            out_shape=shapes,
+            in_specs=[anywhere, anywhere],
+            out_specs=(anywhere, anywhere),
+            scratch_shapes=[
+                pltpu.VMEM((4, 8, 32, 256), F32),
+                pltpu.VMEM((4, 8, 16, 128), F32),
+                pltpu.SemaphoreType.DMA((2, 5)),
+            ],
+        )(*results)
 
     return jax.shard_map(
         body,

time: 44.8 us -> 43.8 us (0.978)
  local copies, waits for them, and re-layouts: 3.06 us -> 0 us
  Pallas kernels: 40.6 us -> 42.7 us
    unnamed x4 -> x0, local copies, waits for them, and re-layouts: 3.06 us -> none
    pallas_call x1 -> x2, Pallas kernels: 40.6 us -> 42.7 us  [the longest x1 40.6 us: body(): pl.pallas_call(functools.partial(kernel, nz, nx, ny), out_shape=shapes, i...]
where the time goes in v5:
time: 43.8 us; the launch traced here: 43.3 us
  Pallas kernels  42.7 us (97%)
  between operations  0.64 us (1%)
    pallas_call x1, Pallas kernels, body(): pl.pallas_call(functools.partial(kernel, nz, nx, ny), out_shape=shapes, i...  40.6 us
    pallas_call x1, Pallas kernels, body(): pl.pallas_call(store_kernel, out_shape=shapes, in_specs=[anywhere, anywhe...  2.08 us

profile of v5, /device:TPU:6, one launch (start us, length us, event | category | flops | bytes accessed | tf_op | source)
XLA Modules:
  0.0 43.3 jit_solution(9054953146426391894)
XLA Ops:
  0.6 40.6 %shard_map.59 = (f32[4,8,32,256]{3,2,1,0:T(8,128)}, f32[4,8,16,128]{3,2,1,0:T(8,128)}) custom-call(f32[4,8,32,256]{3,2,1,0:T(8,128)} %pot.1, s32[8,32,256]{2,1,0:T(8,128)} %lab.1, f32[16]{0:T(128)} %cond.1, s32[4,4]{1,0:T(4,128)} %elec.1), custom_call_target="tpu_custom_call" | custom-call | tf_op jit(solution)/shard_map/pallas_call | solution.py:690
  41.2 2.1 %shard_map.60 = (f32[4,8,32,256]{3,2,1,0:T(8,128)}, f32[4,8,16,128]{3,2,1,0:T(8,128)}) custom-call(f32[4,8,32,256]{3,2,1,0:T(8,128)} %get-tuple-element.4.relaxed, f32[4,8,16,128]{3,2,1,0:T(8,128)} %get-tuple-element.5.restricted), custom_call_target="tpu_custom_call" | custom-call | tf_op jit(solution)/shard_map/pallas_call | solution.py:731

commit v6 on v5

--- a/solution.py
+++ b/solution.py
@@ -134,27 +134,32 @@
         return (
             remote(xp.at[t, 0, :, 0:n], xh.at[t, 1, :, 0:n], xs.at[t, 0], xr.at[t, 1], west),
             remote(xp.at[t, 1, :, 0:n], xh.at[t, 0, :, 0:n], xs.at[t, 1], xr.at[t, 0], east),
-            remote(yp.at[t, 0], yh.at[t, 1], ys.at[t, 0], yr.at[t, 1], south),
-            remote(yp.at[t, 1], yh.at[t, 0], ys.at[t, 1], yr.at[t, 0], north),
+        )
+
+    def y_copies(t, g):
+        return (
+            remote(yp.at[t, g, 0], yh.at[t, g, 1], ys.at[t, g, 0], yr.at[t, g, 1], south),
+            remote(yp.at[t, g, 1], yh.at[t, g, 0], ys.at[t, g, 1], yr.at[t, g, 0], north),
         )
 
     lat = [lateral_copies(t) for t in range(3)]
+    laty = [[y_copies(t, g) for g in range(2)] for t in range(3)]
 
     def send_x(t):
         start(lat[t][0], has_w)
         start(lat[t][1], has_e)
 
-    def send_y(t):
-        start(lat[t][2])
-        start(lat[t][3])
+    def send_y(t, g):
+        for copy in laty[t][g]:
+            start(copy)
 
     def wait_x(t):
         pl.when(has_e)(lat[t][0].wait_recv)
         pl.when(has_w)(lat[t][1].wait_recv)
 
-    def wait_y(t):
-        lat[t][2].wait_recv()
-        lat[t][3].wait_recv()
+    def wait_y(t, g):
+        for copy in laty[t][g]:
+            copy.wait_recv()
 
     def pack_sigma(z, acc):
         acc_s, acc_n = acc
@@ -187,16 +192,19 @@
         return acc_s, acc_n
 
     acc = loop(8, pack_pot, acc)
-    yp[0, 0], yp[0, 1] = acc
+    for d in range(2):
+        yp[0, 0, d] = acc[d][8:24]
+        yp[0, 1, d] = jnp.concatenate([acc[d][0:8], acc[d][24:32]], 0)
     pl.semaphore_wait(
         barrier,
         nz + 1 + has_w.astype(jnp.int32) + has_e.astype(jnp.int32),
     )
 
-    send_x(0)
     start(to_above, has_u)
     start(to_below, has_d)
-    send_y(0)
+    send_y(0, 0)
+    send_y(0, 1)
+    send_x(0)
 
     here = jnp.where(p == 0, 4.0 * ASPECT, 0.0).astype(F32)
     row32 = lax.broadcasted_iota(jnp.int32, (32, 128), 0)
@@ -226,8 +234,8 @@
         )
 
     def neighbours(g, t, k, v):
-        halo_s = roll(centre(g, yh[t, 0]), lax.rem(128 - k, 128), 1)
-        halo_n = roll(centre(g, yh[t, 1]), 127 - k, 1)
+        halo_s = roll(yh[t, g, 0], lax.rem(128 - k, 128), 1)
+        halo_n = roll(yh[t, g, 1], 127 - k, 1)
         ctr = [centre(g, v[c]) for c in range(2)]
         sn = south_north(ctr[0], ctr[1], halo_s, halo_n)
         res = []
@@ -455,7 +463,7 @@
                 kx[g, 1, c] = k
                 kx[g, 2, c] = k * b3r[g, 1, c]
                 kx[g, 3, c] = k * b3r[g, 2, c]
-                for i in range(4, 9):
+                for i in range(4, 7):
                     kx[g, i, c] = jnp.zeros((16, 128), F32)
 
     def cross_send(g, h):
@@ -509,12 +517,8 @@
         return loop(8, body, acc + (first,))[:2]
 
     def pack_y(t, g, acc):
-        for d in range(2):
-            if g == 0:
-                yp[t + 1, d, 8:24] = acc[d]
-            else:
-                yp[t + 1, d, 0:8] = acc[d][0:8]
-                yp[t + 1, d, 24:32] = acc[d][8:16]
+        yp[t + 1, g, 0], yp[t + 1, g, 1] = acc
+        send_y(t + 1, g)
 
     def put(ref, g, s, z, c, v):
         if g == 0:
@@ -547,7 +551,7 @@
 
     empty = (jnp.zeros((16, 128), F32),) * 2
 
-    wait_y(0)
+    wait_y(0, 0)
     pl.when(has_d)(to_above.wait_recv)
     pl.when(has_u)(to_below.wait_recv)
     setup(0)
@@ -555,6 +559,7 @@
     for h in range(2):
         forward(0, 0, h, load_pot)
         end_send(0, h)
+    wait_y(0, 1)
     wait_x(0)
     setup(1)
     end_factor(1)
@@ -573,30 +578,34 @@
         for h in range(2):
             end_solve(g, h)
             acc = backward(0, g, h, emit_first(g), acc)
+        if g == 1:
+            send_x(1)
         pack_y(0, g, acc)
-    send_x(1)
-    send_y(1)
     for g in range(2):
         mid_extra(g)
-    for g in range(2):
-        end_extra(g)
-
-    wait_y(1)
+
+    @pl.when(is_end)
+    def _():
+        kx[:, 7:9] = jnp.zeros((2, 2, 2, 16, 128), F32)
+
+    wait_y(1, 0)
     for h in range(2):
         forward(0, 1, h, load_first)
         cross_send(0, h)
+    wait_y(1, 1)
     wait_x(1)
     for h in range(2):
         forward(1, 1, h, load_first)
         cross_send(1, h)
     for g in range(2):
+        end_extra(g)
         acc = empty
         for h in range(2):
             cross_solve(g, h)
             acc = backward(1, g, h, emit_relaxed(g), acc)
+        if g == 1:
+            send_x(2)
         pack_y(1, g, acc)
-    send_x(2)
-    send_y(2)
     out_cp = [
         pltpu.make_async_copy(on.at[:, :, c], out.at[:, :, :, c * 128:(c + 1) * 128], loc.at[0, c])
         for c in range(2)
@@ -638,8 +647,9 @@
 
         loop(8, body, 0)
 
-    wait_y(2)
+    wait_y(2, 0)
     defect(0)
+    wait_y(2, 1)
     wait_x(2)
     defect(1)
     co_cp = pltpu.make_async_copy(co, coarse, loc.at[1, 0])
@@ -703,8 +713,8 @@
                 pltpu.VMEM((10, 2, 32, 128), F32),
                 pltpu.VMEM((3, 2, 2, 40, 128), F32),
                 pltpu.VMEM((3, 2, 2, 40, 128), F32),
-                pltpu.VMEM((3, 2, 32, 128), F32),
-                pltpu.VMEM((3, 2, 32, 128), F32),
+                pltpu.VMEM((3, 2, 2, 16, 128), F32),
+                pltpu.VMEM((3, 2, 2, 16, 128), F32),
                 pltpu.VMEM((4, 2, 32, 128), F32),
                 coef, coef, coef, coef, coef, coef, coef, coef, coef,
                 pltpu.VMEM((2, 4, 2, 16, 128), F32),
@@ -720,7 +730,7 @@
                 pltpu.VMEM((2, 2, 3, 2, 2, 16, 128), F32),
                 pltpu.VMEM((2, 9, 2, 16, 128), F32),
                 dma((2, 2)), dma((2,)), dma((2,)),
-                dma((3, 2)), dma((3, 2)), dma((3, 2)), dma((3, 2)),
+                dma((3, 2)), dma((3, 2)), dma((3, 2, 2)), dma((3, 2, 2)),
                 dma((2, 2, 3)), dma((2, 2, 3)), dma((2, 3)), dma((2, 3)),
                 dma((2, 2, 3)), dma((2, 2, 3)),
             ],

time: 43.8 us -> 42.5 us (0.970)
  Pallas kernels: 42.7 us -> 41.7 us
    pallas_call x1, Pallas kernels: 40.6 us -> 39.6 us  [body(): pl.pallas_call(functools.partial(kernel, nz, nx, ny), out_shape=shapes, i...]
where the time goes in v6:
time: 42.5 us; the launch traced here: 42.3 us
  Pallas kernels  41.7 us (98%)
  between operations  0.64 us (2%)
    pallas_call x1, Pallas kernels, body(): pl.pallas_call(functools.partial(kernel, nz, nx, ny), out_shape=shapes, i...  39.6 us
    pallas_call x1, Pallas kernels, body(): pl.pallas_call(store_kernel, out_shape=shapes, in_specs=[anywhere, anywhe...  2.08 us

profile of v6, /device:TPU:6, one launch (start us, length us, event | category | flops | bytes accessed | tf_op | source)
XLA Modules:
  0.0 42.3 jit_solution(13121727771623994674)
XLA Ops:
  0.6 39.6 %shard_map.59 = (f32[4,8,32,256]{3,2,1,0:T(8,128)}, f32[4,8,16,128]{3,2,1,0:T(8,128)}) custom-call(f32[4,8,32,256]{3,2,1,0:T(8,128)} %pot.1, s32[8,32,256]{2,1,0:T(8,128)} %lab.1, f32[16]{0:T(128)} %cond.1, s32[4,4]{1,0:T(4,128)} %elec.1), custom_call_target="tpu_custom_call" | custom-call | tf_op jit(solution)/shard_map/pallas_call | solution.py:700
  40.2 2.1 %shard_map.60 = (f32[4,8,32,256]{3,2,1,0:T(8,128)}, f32[4,8,16,128]{3,2,1,0:T(8,128)}) custom-call(f32[4,8,32,256]{3,2,1,0:T(8,128)} %get-tuple-element.4.relaxed, f32[4,8,16,128]{3,2,1,0:T(8,128)} %get-tuple-element.5.restricted), custom_call_target="tpu_custom_call" | custom-call | tf_op jit(solution)/shard_map/pallas_call | solution.py:741

commit v7 on v6

--- a/solution.py
+++ b/solution.py
@@ -572,15 +572,16 @@
             mid_forward(g, h)
     for g in range(2):
         mid_match(g)
-        acc = empty
         for h in range(2):
             mid_solve(g, h)
+    for g in range(2):
+        acc = empty
         for h in range(2):
             end_solve(g, h)
             acc = backward(0, g, h, emit_first(g), acc)
+        pack_y(0, g, acc)
         if g == 1:
             send_x(1)
-        pack_y(0, g, acc)
     for g in range(2):
         mid_extra(g)
 
@@ -603,9 +604,9 @@
         for h in range(2):
             cross_solve(g, h)
             acc = backward(1, g, h, emit_relaxed(g), acc)
+        pack_y(1, g, acc)
         if g == 1:
             send_x(2)
-        pack_y(1, g, acc)
     out_cp = [
         pltpu.make_async_copy(on.at[:, :, c], out.at[:, :, :, c * 128:(c + 1) * 128], loc.at[0, c])
         for c in range(2)

time: 42.5 us -> 42.6 us (level)
  no operation moved by 1% of the time
where the time goes in v7:
time: 42.6 us; the launch traced here: 42.5 us
  Pallas kernels  41.8 us (98%)
  between operations  0.64 us (2%)
    pallas_call x1, Pallas kernels, body(): pl.pallas_call(functools.partial(kernel, nz, nx, ny), out_shape=shapes, i...  39.7 us
    pallas_call x1, Pallas kernels, body(): pl.pallas_call(store_kernel, out_shape=shapes, in_specs=[anywhere, anywhe...  2.08 us

profile of v7, /device:TPU:6, one launch (start us, length us, event | category | flops | bytes accessed | tf_op | source)
XLA Modules:
  0.0 42.5 jit_solution(968719170776107566)
XLA Ops:
  0.6 39.7 %shard_map.59 = (f32[4,8,32,256]{3,2,1,0:T(8,128)}, f32[4,8,16,128]{3,2,1,0:T(8,128)}) custom-call(f32[4,8,32,256]{3,2,1,0:T(8,128)} %pot.1, s32[8,32,256]{2,1,0:T(8,128)} %lab.1, f32[16]{0:T(128)} %cond.1, s32[4,4]{1,0:T(4,128)} %elec.1), custom_call_target="tpu_custom_call" | custom-call | tf_op jit(solution)/shard_map/pallas_call | solution.py:701
  40.4 2.1 %shard_map.60 = (f32[4,8,32,256]{3,2,1,0:T(8,128)}, f32[4,8,16,128]{3,2,1,0:T(8,128)}) custom-call(f32[4,8,32,256]{3,2,1,0:T(8,128)} %get-tuple-element.4.relaxed, f32[4,8,16,128]{3,2,1,0:T(8,128)} %get-tuple-element.5.restricted), custom_call_target="tpu_custom_call" | custom-call | tf_op jit(solution)/shard_map/pallas_call | solution.py:742
